TPU v7x, 32 devices: a whole 2x2x4 slice. The times are simulated.
32 devices in a mesh: grp: 8 (over y, x, core), shard: 4 (over z).
Axes of the slice: x: 2, y: 2, z: 4, core: 2. Of those that a mesh axis runs over, the one named last changes fastest.
Arguments:
- left_table: float32 [131072, 400], P(('grp', 'shard')), may hold values from -2.4 to 2.4
- right_table: float32 [131072, 400], P(('grp', 'shard')), may hold values from -2.4 to 2.4
- left_state: float32 [131072], P(('grp', 'shard')), may hold values from 0.1 to 4
- right_state: float32 [131072], P(('grp', 'shard')), may hold values from 0.1 to 4
- relations: float32 [1345, 400], replicated, may hold values from -4.2 to 4.2
- relation_state: float32 [1345], replicated, may hold values from 0.1 to 100000
- source_rows: int32 [288, 1000], P(('grp', 'shard')), may hold values from 0 to 4095
- relation_ids: int32 [288, 1000], P(('grp', 'shard')), may hold values from 0 to 1344
- target_rows: int32 [288, 1000], P(('grp', 'shard')), may hold values from 0 to 4095
- negative_rows: int32 [288, 1000], P(('grp', 'shard')), may hold values from 0 to 4095
- span_sizes: int32 [32, 9], P(('grp', 'shard')), may hold values from 1 to 1000, 6750 in all within a row
Outputs:
- new_left: float32 [131072, 400], P(('grp', 'shard'))
- new_left_state: float32 [131072], P(('grp', 'shard'))
- new_right: float32 [131072, 400], P(('grp', 'shard'))
- new_right_state: float32 [131072], P(('grp', 'shard'))
- new_relations: float32 [1345, 400], replicated
- new_relation_state: float32 [1345], replicated
Inputs may be any that keep to these rules, and one draw needn't show every extreme that they name: `source_rows`: local row ids of the device's own source-side rows. `target_rows`: local row ids of the device's own target-side rows. `negative_rows`: negative j of a span names a local row of device j // 250 of the same group; rows may repeat. The first span_sizes edges of a span are live.
All inputs are finite; a program needn't handle non-finite values.
Results may differ from a plain program's by a relative error of at most 0.0017.
Values may be sent and summed in bfloat16 or wider, within the bound.
No kernel may reach another device: no remote copies, remote signals or barrier semaphores. Data moves between devices by JAX's collectives and lax.ppermute only.
A program may use at most 256 MiB of HBM per device.

v0:
```python
import jax
import jax.numpy as jnp
from jax import lax
from jax.sharding import PartitionSpec as P

ROUND = 5


LEARN_RATE = 0.1
EPSILON = 1e-08


def passed_along(block, axis, distance):
    devices = range(lax.axis_size(axis))
    route = [((i - distance) % len(devices), i) for i in devices]
    return lax.ppermute(block, axis, route)


def complex_mul(left, right):
    middle = left.shape[-1] // 2
    left_real, left_imag = (left[..., :middle], left[..., middle:])
    right_real, right_imag = (right[..., :middle], right[..., middle:])
    return jnp.concatenate(
        [
            left_real * right_real - left_imag * right_imag,
            left_real * right_imag + left_imag * right_real,
        ],
        -1,
    )


def conj_mul(grad, other):
    middle = grad.shape[-1] // 2
    grad_real, grad_imag = (grad[..., :middle], grad[..., middle:])
    other_real, other_imag = (other[..., :middle], other[..., middle:])
    return jnp.concatenate(
        [
            grad_real * other_real + grad_imag * other_imag,
            grad_imag * other_real - grad_real * other_imag,
        ],
        -1,
    )


def span_terms(source, relation, target, negatives, weights):
    product = complex_mul(source, relation)
    product_b = product.astype(jnp.bfloat16)
    positive = jnp.sum(product * target, -1)
    scores = lax.dot_general(
        product_b, negatives, (((1,), (1,)), ((), ())), preferred_element_type=jnp.float32
    )
    pos_grad = -jax.nn.sigmoid(-positive) * weights
    neg_grad = (jax.nn.sigmoid(scores) * weights[:, None]).astype(jnp.bfloat16)
    grad_product = pos_grad[:, None] * target + jnp.dot(
        neg_grad, negatives, preferred_element_type=jnp.float32
    )
    grad_target = pos_grad[:, None] * product
    grad_negatives = lax.dot_general(
        neg_grad, product_b, (((0,), (0,)), ((), ())), preferred_element_type=jnp.float32
    ).astype(jnp.bfloat16)
    grad_source = conj_mul(grad_product, relation)
    grad_relation = conj_mul(grad_product, source)
    return (grad_source, grad_relation, grad_target, grad_negatives)


def row_adagrad(table, state, grad):
    new_state = state + jnp.mean(grad * grad, -1)
    return (table - LEARN_RATE * grad / (jnp.sqrt(new_state)[:, None] + EPSILON), new_state)


def local(
    left_table,
    right_table,
    left_state,
    right_state,
    relations,
    relation_state,
    source_rows,
    relation_ids,
    target_rows,
    negative_rows,
    span_sizes,
):
    shards = lax.axis_size("shard")
    spans, span_len = source_rows.shape
    neg_count = negative_rows.shape[1]
    neg_per = neg_count // shards
    width = left_table.shape[1]
    asked = lax.all_to_all(
        negative_rows.reshape(spans, shards, neg_per),
        "shard",
        split_axis=1,
        concat_axis=1,
        tiled=True,
    )
    served = right_table[asked].astype(jnp.bfloat16)
    fetched = lax.all_to_all(served, "shard", split_axis=1, concat_axis=1, tiled=True).reshape(
        spans, neg_count, width
    )
    positions = jnp.arange(span_len, dtype=jnp.int32)

    def step(carry, inputs):
        grad_left, grad_right, grad_rel = carry
        sources, kinds, targets, negatives, live = inputs
        weights = (positions < live).astype(jnp.float32)
        source = left_table[sources]
        relation = relations[kinds]
        target = right_table[targets]
        grad_source, grad_relation, grad_target, grad_negatives = span_terms(
            source, relation, target, negatives, weights
        )
        grad_left = grad_left.at[sources].add(grad_source)
        grad_right = grad_right.at[targets].add(grad_target)
        grad_rel = grad_rel.at[kinds].add(grad_relation)
        return ((grad_left, grad_right, grad_rel), grad_negatives)

    start = (
        jnp.zeros(left_table.shape, jnp.float32),
        jnp.zeros(right_table.shape, jnp.float32),
        jnp.zeros(relations.shape, jnp.float32),
    )
    totals, neg_grads = lax.scan(
        step, start, (source_rows, relation_ids, target_rows, fetched, span_sizes[0])
    )
    grad_left, grad_right, grad_rel = totals
    new_left, new_left_state = row_adagrad(left_table, left_state, grad_left)
    returned = lax.all_to_all(
        neg_grads.reshape(spans, shards, neg_per, width),
        "shard",
        split_axis=1,
        concat_axis=1,
        tiled=True,
    )
    grad_right = grad_right.at[asked.reshape(-1)].add(
        returned.reshape(-1, width).astype(jnp.float32)
    )
    rel_total = lax.psum(grad_rel, ("grp", "shard"))
    new_right, new_right_state = row_adagrad(right_table, right_state, grad_right)
    new_relations, new_relation_state = row_adagrad(relations, relation_state, rel_total)
    moved = passed_along((new_left, new_left_state, new_right, new_right_state), "grp", ROUND)
    return (moved[0], moved[1], moved[2], moved[3], new_relations, new_relation_state)


def solution(mesh):
    placed = (
        P(("grp", "shard"), None),
        P(("grp", "shard"), None),
        P(("grp", "shard")),
        P(("grp", "shard")),
        P(),
        P(),
        P(("grp", "shard"), None),
        P(("grp", "shard"), None),
        P(("grp", "shard"), None),
        P(("grp", "shard"), None),
        P(("grp", "shard"), None),
    )
    return jax.shard_map(
        local,
        mesh=mesh,
        in_specs=placed,
        out_specs=(
            P(("grp", "shard"), None),
            P(("grp", "shard")),
            P(("grp", "shard"), None),
            P(("grp", "shard")),
            P(),
            P(),
        ),
        check_vma=False,
    )
```

profile of v0, /device:TPU:1, one launch (start us, length us, event | category | flops | bytes accessed | tf_op | source)
XLA Modules:
  0.0 1837.0 jit_solution(10612433512499536425)
XLA Ops:
  22.9 30.1 %gather_fusion.3 = bf16[9000,400]{1,0:T(8,128)(2,1)} fusion(f32[4096,400]{1,0:T(8,128)} %copy.173, s32[9216]{0:T(1024)S(1)} %pad_clamp_fusion.3), kind=kCustom, calls=%fused_computation.3 | custom fusion | bytes 14436000 | tf_op jit(solution)/shard_map/gather | solution.py:96
  53.0 11.3 copy.168
  64.3 18.2 reshape.229
  105.8 150.2 %all-to-all-done.1 = bf16[9,4,250,400]{2,3,0,1:T(8,128)(2,1)} async-done(((bf16[9,4,250,400]{2,3,0,1:T(8,128)(2,1)}), bf16[9,4,250,400]{2,3,0,1:T(8,128)(2,1)}, u32[]{:S(2)}, u32[]{:S(2)}) %all-to-all-start.1) | async-done | bytes 7200032 | tf_op jit(solution)/shard_map/all_to_all | solution.py:97
  256.0 11.3 copy.184
  267.3 12.4 reshape.245
  288.7 1021.1 %while.17 = (s32[]{:T(128)}, f32[4096,400]{1,0:T(8,128)}, f32[4096,400]{1,0:T(8,128)}, f32[1345,400]{1,0:T(8,128)S(1)}, bf16[9,1000,400]{1,2,0:T(8,128)(2,1)}, /...) while((s32[]{:T(128)}, f32[4096,400]{1,0:T(8,128)}, ...), condition=%wide.region_5.6_spmd.clone, body=%wide.region_0.5_spmd.clone.sunk | while | flops 2417018112 | bytes 130692728 | solution.py:122
  291.9 8.6 gather_fusion.1
  318.6 8.6 gather_fusion
  373.9 13.8 scatter_fusion
  387.7 13.8 scatter_fusion.1
  404.4 8.6 gather_fusion.1
  431.1 8.6 gather_fusion
  486.3 13.8 scatter_fusion
  500.1 13.8 scatter_fusion.1
  516.8 8.6 gather_fusion.1
  543.5 8.6 gather_fusion
  598.8 13.8 scatter_fusion
  612.6 13.8 scatter_fusion.1
  629.3 8.6 gather_fusion.1
  656.0 8.6 gather_fusion
  711.3 13.8 scatter_fusion
  725.1 13.8 scatter_fusion.1
  741.7 8.6 gather_fusion.1
  768.4 8.6 gather_fusion
  823.7 13.8 scatter_fusion
  837.5 13.8 scatter_fusion.1
  854.2 8.6 gather_fusion.1
  936.2 13.8 scatter_fusion
  950.1 13.8 scatter_fusion.1
  966.7 8.6 gather_fusion.1
  1048.7 13.8 scatter_fusion
  1062.5 13.8 scatter_fusion.1
  1079.2 8.6 gather_fusion.1
  1105.9 8.6 gather_fusion
  1161.2 13.8 scatter_fusion
  1175.0 13.8 scatter_fusion.1
  1191.7 8.6 gather_fusion.1
  1273.6 13.8 scatter_fusion
  1287.5 13.8 scatter_fusion.1
  1309.8 18.1 reshape.161
  1345.3 10.0 divide_subtract_fusion.1
  1367.3 134.3 %all-to-all-done.2 = bf16[9,4,250,400]{2,3,0,1:T(8,128)(2,1)} async-done(((bf16[9,4,250,400]{2,3,0,1:T(8,128)(2,1)}), bf16[9,4,250,400]{2,3,0,1:T(8,128)(2,1)}, u32[]{:S(2)}, u32[]{:S(2)}) %all-to-all-start.2) | async-done | bytes 7200032 | tf_op jit(solution)/shard_map/all_to_all | solution.py:127
  1501.5 12.9 copy.185
  1514.4 16.7 reshape.246
  1531.1 61.8 %scatter_fusion.3 = f32[4096,400]{1,0:T(8,128)} fusion(f32[4096,400]{1,0:T(8,128)} %get-tuple-element.82, s32[9000]{0:T(1024)S(1)} %fusion.18, f32[9000,400]{1,0:T(8,128)} %reshape.246), kind=kCustom, calls=%fused_computation.7 | custom fusion | flops 3600000 | bytes 43236000 | tf_op jit(solution)/shard_map/scatter-add | solution.py:134
  1619.1 73.6 %collective-permute-done.1 = f32[4096]{0:T(1024)S(1)} collective-permute-done((f32[4096]{0:T(1024)S(1)}, f32[4096]{0:T(1024)S(1)}, u32[]{:S(2)}, u32[]{:S(2)}) %collective-permute-start.1) | collective-permute-done | bytes 16416 | tf_op jit(solution)/shard_map/ppermute | solution.py:16
  1692.7 116.5 %all-reduce.2.cloned.1.call-done = f32[1345,400]{0,1:T(8,128)} async-done(((f32[1345,400]{0,1:T(8,128)}), f32[1345,400]{0,1:T(8,128)}) %all-reduce.2.cloned.1.call-update) | async-done | bytes 2152016 | tf_op jit(solution)/shard_map/psum | solution.py:137
  (492 shorter events, 756.5 us)
Async XLA Ops:
  8.7 14.0 all-to-all-start
  22.7 30.3 %copy-start.12 = (s32[9,4,250]{2,0,1:T(8,128)}, s32[9,4,250]{2,0,1:T(8,128)S(1)}, u32[]{:S(2)}) copy-start(s32[9,4,250]{2,0,1:T(8,128)S(1)} %all-to-all-done) | copy-start | bytes 108004
  89.5 5.6 copy-start.9
  89.5 166.5 %all-to-all-start.1 = ((bf16[9,4,250,400]{2,3,0,1:T(8,128)(2,1)}), bf16[9,4,250,400]{2,3,0,1:T(8,128)(2,1)}, u32[]{:S(2)}, u32[]{:S(2)}) async-start(bf16[9,4,250,400]{2,3,0,1:T(8,128)(2,1)} %copy.169), calls=%async_computation.1 | async-start | bytes 14745600 | tf_op jit(solution)/shard_map/all_to_all | solution.py:97
  284.4 4.3 copy-start.17
  343.1 3.8 copy-start.8
  455.6 3.8 copy-start.8
  568.0 3.8 copy-start.8
  571.8 3.1 copy-start.18
  571.9 3.1 copy-start.3
  571.9 3.1 copy-start.4
  571.9 3.1 copy-start.5
  571.9 3.1 copy-start.6
  680.5 3.8 copy-start.8
  793.0 3.8 copy-start.8
  796.8 3.1 copy-start.18
  796.8 3.1 copy-start.3
  796.8 3.1 copy-start.4
  796.8 3.1 copy-start.5
  796.8 3.1 copy-start.6
  905.4 3.8 copy-start.8
  909.3 3.1 copy-start.18
  909.3 3.1 copy-start.3
  909.3 3.1 copy-start.4
  909.3 3.1 copy-start.5
  909.3 3.1 copy-start.6
  1018.0 3.8 copy-start.8
  1130.4 3.8 copy-start.8
  1134.2 3.1 copy-start.18
  1134.2 3.1 copy-start.3
  1134.2 3.1 copy-start.4
  1134.3 3.1 copy-start.5
  1134.3 3.1 copy-start.6
  1242.9 3.8 copy-start.8
  1246.7 3.1 copy-start.18
  1335.1 5.7 copy-start.13
  1335.1 166.4 %all-to-all-start.2 = ((bf16[9,4,250,400]{2,3,0,1:T(8,128)(2,1)}), bf16[9,4,250,400]{2,3,0,1:T(8,128)(2,1)}, u32[]{:S(2)}, u32[]{:S(2)}) async-start(bf16[9,4,250,400]{2,3,0,1:T(8,128)(2,1)} %copy.178), calls=%async_computation.2 | async-start | bytes 14745600 | tf_op jit(solution)/shard_map/all_to_all | solution.py:127
  1340.7 468.4 %all-reduce.2.cloned.1.call-start = ((), (), s32[]{:S(2)}) async-start(), calls=%async_computation.3 | async-start | bytes 4505600 | tf_op jit(solution)/shard_map/psum | solution.py:137
  1341.1 4.1 copy-start.14
  1363.8 452.1 %collective-permute-start = (f32[4096,400]{0,1:T(8,128)}, f32[4096,400]{0,1:T(8,128)}, u32[]{:S(2)}, u32[]{:S(2)}) collective-permute-start(f32[4096,400]{0,1:T(8,128)} %copy.176), channel_id=1, source_target_pairs={{12,0},{16,4},{20,8},{24,12},{28,16},{0,20},{4,24},{8,28},{13,1},{... | collective-permute-start | bytes 19660808 | tf_op jit(solution)/shard_map/ppermute | solution.py:16
  1592.9 4.2 copy-start.15
  1592.9 5.8 copy-start
  1613.4 202.5 %collective-permute-start.2 = (f32[4096,400]{0,1:T(8,128)}, f32[4096,400]{0,1:T(8,128)}, u32[]{:S(2)}, u32[]{:S(2)}) collective-permute-start(f32[4096,400]{0,1:T(8,128)} %copy.182), channel_id=1, source_target_pairs={{12,0},{16,4},{20,8},{24,12},{28,16},{0,20},{4,24},{8,28},{13,1},{... | collective-permute-start | bytes 19660808 | tf_op jit(solution)/shard_map/ppermute | solution.py:16
  1619.0 192.1 %copy-start.16 = (f32[1345]{0:T(1024)S(1)}, f32[1345]{0:T(1024)}, u32[]{:S(2)}) copy-start(f32[1345]{0:T(1024)} %param.18) | copy-start | bytes 16144
  1619.0 195.2 %copy-start.10 = (f32[1345,400]{0,1:T(8,128)S(1)}, f32[1345,400]{0,1:T(8,128)}, u32[]{:S(2)}) copy-start(f32[1345,400]{0,1:T(8,128)} %param.17) | copy-start | bytes 6456004
  1619.0 73.6 %collective-permute-start.1 = (f32[4096]{0:T(1024)S(1)}, f32[4096]{0:T(1024)S(1)}, u32[]{:S(2)}, u32[]{:S(2)}) collective-permute-start(f32[4096]{0:T(1024)S(1)} %get-tuple-element.247), channel_id=1, source_target_pairs={{12,0},{16,4},{20,8},{24,12},{28,16},{0,20},{4,24},{8,28},{13,1},{... | collective-permute-start | bytes 49160 | tf_op jit(solution)/shard_map/ppermute | solution.py:16
  1809.2 5.0 copy-start.11
  1811.8 4.1 collective-permute-start.3
  (51 other events, 117.1 us)
Sparse Core Ops, SparseCore 0:
  1619.2 189.9 all-reduce.1
where the time goes:
time: 1850 us; the launch traced here: 1840 us
  local copies, waits for them, and re-layouts  684 us (37%)
  other arithmetic  530 us (29%)
  waiting for transfers between devices  475 us (26%)
  matrix products  97.1 us (5%)
  starting transfers between devices  26.2 us (1%)
    all_to_all x1, waiting for transfers between devices, local(): lax.all_to_all(served, 'shard', split_axis=1, concat_axis=1, tiled=True)  150 us
    all_to_all x1, waiting for transfers between devices, local(): lax.all_to_all(neg_grads.reshape(spans, shards, neg_per, width), 'shard',...  134 us
    scatter-add x9, other arithmetic, step(): grad_right = grad_right.at[targets].add(grad_target)  124 us
    scatter-add x9, other arithmetic, step(): grad_left = grad_left.at[sources].add(grad_source)  124 us
    psum x1, waiting for transfers between devices, local(): rel_total = lax.psum(grad_rel, ('grp', 'shard'))  117 us
    gather x18, local copies, waits for them, and re-layouts, step(): target = right_table[targets]  103 us
    while x198, local copies, waits for them, and re-layouts  89.4 us
    gather x9, local copies, waits for them, and re-layouts, step(): source = left_table[sources]  77.7 us
  transfers between devices with their start and end apart: 8, of which 4 were waited for; matrix products, arithmetic and copies ran while one was open for 9% of the time, Pallas kernels for 0%

commit v1 on v0

v1 whole, which is shorter than its diff:
```python
import functools

import jax
import jax.numpy as jnp
from jax import lax
from jax.experimental import pallas as pl
from jax.experimental.pallas import tpu as pltpu
from jax.sharding import PartitionSpec as P

ROUND = 5
LEARN_RATE = 0.1
EPSILON = 1e-08
LANES = 128
TILE = 256
GROUP = 16
PITCH = 5
CODE = 32767.0
VMEM_LIMIT = 58 * 1024 * 1024
F32 = jnp.float32
BF16 = jnp.bfloat16


def round_up(n, m):
    return -(-n // m) * m


def params(**kw):
    return pltpu.CompilerParams(vmem_limit_bytes=VMEM_LIMIT, **kw)


def cost(flops, nbytes):
    return pl.CostEstimate(flops=int(flops), bytes_accessed=int(nbytes), transcendentals=0)


def whole(shape):
    return pl.BlockSpec(shape, lambda *_: (0,) * len(shape), pipeline_mode=pl.Buffered(1))


def parts_of(width):
    half = width // 2
    rest = half - LANES
    return ((0, LANES), (LANES, rest), (half, LANES), (half + LANES, rest))


def split_kernel(t_ref, o_ref, *, width, cols):
    for b in range(cols // LANES):
        for j, (start, size) in enumerate(parts_of(width)):
            x = t_ref[start : start + size, b * LANES : (b + 1) * LANES]
            if size < LANES:
                x = jnp.concatenate([x, jnp.zeros((LANES - size, LANES), F32)], 0)
            o_ref[pl.ds(4 * LANES * b + j, LANES, stride=4), :] = x.T


def split_rows(table_t, cols):
    width, rows = table_t.shape
    return pl.pallas_call(
        functools.partial(split_kernel, width=width, cols=cols),
        grid=(rows // cols,),
        in_specs=[pl.BlockSpec((width, cols), lambda i: (0, i))],
        out_specs=pl.BlockSpec((4 * cols, LANES), lambda i: (i, 0)),
        out_shape=jax.ShapeDtypeStruct((4 * rows, LANES), F32),
        compiler_params=params(),
        cost_estimate=cost(0, 4 * rows * (width + 512)),
        name="split_rows",
    )(table_t)


def serve_kernel(idx_ref, t_ref, o_ref, tb, *, rows, step):
    @pl.when((pl.program_id(0) == 0) & (pl.program_id(1) == 0))
    def _():
        for k in range(0, rows, step):
            tb[:, k : k + step] = t_ref[:, k : k + step].astype(BF16)

    idx = idx_ref[0, 0].astype(jnp.int16)
    lanes = idx.shape[-1]
    row = lax.broadcasted_iota(jnp.int16, (step, lanes), 0)
    one, zero = jnp.ones((), BF16), jnp.zeros((), BF16)
    acc = jnp.zeros((t_ref.shape[0], lanes), F32)
    for k in range(0, rows, step):
        hot = jnp.where(row == idx - k, one, zero)
        acc += jnp.dot(tb[:, k : k + step], hot, preferred_element_type=F32)
    o_ref[0] = acc.astype(BF16)


def serve(asked, table_t, first, count):
    shards, spans, _, npp = asked.shape
    width, rows = table_t.shape
    return pl.pallas_call(
        functools.partial(serve_kernel, rows=rows, step=512),
        grid=(shards, count),
        in_specs=[
            pl.BlockSpec((1, 1, 1, npp), lambda q, s: (q, s + first, 0, 0)),
            whole((width, rows)),
        ],
        out_specs=pl.BlockSpec((1, width, npp), lambda q, s: (q, 0, s)),
        out_shape=jax.ShapeDtypeStruct((shards, width, count * npp), BF16),
        scratch_shapes=[pltpu.VMEM((width, rows), BF16)],
        compiler_params=params(),
        cost_estimate=cost(2 * width * rows * shards * count * npp, 4 * width * rows),
        name="serve",
    )(asked, table_t)


def four(i):
    return pl.ds(pl.multiple_of(4 * i, 4), 4)


def staged(first, u):
    return pl.ds(PITCH * (first + u), 4)


def column(first, j, size):
    return pl.ds(pl.multiple_of(PITCH * first, 8) + j, size, stride=PITCH)


def add_rows(jobs, span, edge, first, at, n):
    done = []
    for idx, total, stage in jobs:
        ids = [idx[span, edge + u] for u in range(n)]
        grads = [stage[staged(first, at + u), :] for u in range(n)]
        sums = [total[four(i), :] for i in ids]
        for k in range(n):
            new = sums[k] + grads[k]
            for j in range(k):
                new += grads[j] * jnp.where(ids[j] == ids[k], 1.0, 0.0)
            done.append((total, ids[k], new))
    for total, i, new in done:
        total[four(i), :] = new


def tiles_of(count):
    return (count + TILE - 1) // TILE


def edge_kernel(
    src_idx, rel_idx, tgt_idx, live,
    left4, rel4, right4,
    p_ref, pt_ref, src_ref, rel_ref, tgt_ref, gt_ref,
    st_s, st_r, st_t,
):
    span = pl.program_id(0)
    count = live[span]

    def one_tile(tile, _):
        base = pl.multiple_of(tile * TILE, TILE)

        @pl.loop(0, TILE, step=GROUP)
        def _(r0):
            for v in range(0, GROUP, 8):
                first = r0 + v
                ats = [staged(first, u) for u in range(8)]
                for idx, table, stage in (
                    (src_idx, left4, st_s), (rel_idx, rel4, st_r), (tgt_idx, right4, st_t),
                ):
                    rows = [table[four(idx[span, base + first + u]), :] for u in range(8)]
                    for at, row in zip(ats, rows):
                        stage[at, :] = row

        sub = 32
        lane = lax.broadcasted_iota(jnp.int32, (sub, LANES), 1)
        low = lane < 72

        @pl.loop(0, TILE, step=sub)
        def _(r0):
            r0 = pl.multiple_of(r0, sub)
            here = pl.ds(pl.multiple_of(base + r0, sub), sub)
            s, r, t = (
                [st[column(r0, j, sub), :] for j in range(4)]
                for st in (st_s, st_r, st_t)
            )
            re0 = s[0] * r[0] - s[2] * r[2]
            re1 = s[1] * r[1] - s[3] * r[3]
            im0 = s[0] * r[2] + s[2] * r[0]
            im1 = s[1] * r[3] + s[3] * r[1]
            prod = (re0, re1, im0, im1)
            score = jnp.sum(re0 * t[0] + re1 * t[1] + im0 * t[2] + im1 * t[3], -1, keepdims=True)
            row = lax.broadcasted_iota(jnp.int32, (sub, 1), 0) + (base + r0)
            weight = jnp.where(row < count, 1.0, 0.0)
            grad = -(0.5 - 0.5 * jnp.tanh(0.5 * score)) * weight
            for j in range(4):
                src_ref[0, here, j * LANES : (j + 1) * LANES] = s[j]
                rel_ref[0, here, j * LANES : (j + 1) * LANES] = r[j]
                tgt_ref[0, here, j * LANES : (j + 1) * LANES] = grad * t[j]
                gt_ref[column(base + r0, j, sub), :] = grad * prod[j]
            r_a = pltpu.roll(im0, 72, 1)
            r_b = pltpu.roll(im1, 72, 1)
            natural = (
                re0, jnp.where(low, re1, r_a), jnp.where(low, r_a, r_b), jnp.where(low, r_b, 0.0),
            )
            for j in range(4):
                p_ref[0, here, j * LANES : (j + 1) * LANES] = natural[j].astype(BF16)

        width = pt_ref.shape[1]
        here = pl.ds(base, TILE)
        for j in range(4):
            size = min(LANES, width - j * LANES)
            x = p_ref[0, here, j * LANES : (j + 1) * LANES].T
            pt_ref[0, j * LANES : j * LANES + size, here] = x[:size]
        return 0

    lax.fori_loop(0, tiles_of(count), one_tile, 0)


def edges(src_idx, rel_idx, tgt_idx, live, left4, rel4, right4, width):
    spans, length = src_idx.shape
    row_spec = pl.BlockSpec((1, length, 512), lambda s, *_: (s, 0, 0))
    rows_f32 = jax.ShapeDtypeStruct((spans, length, 512), F32)
    return pl.pallas_call(
        edge_kernel,
        grid_spec=pltpu.PrefetchScalarGridSpec(
            num_scalar_prefetch=4,
            grid=(spans,),
            in_specs=[whole(left4.shape), whole(rel4.shape), whole(right4.shape)],
            out_specs=[
                row_spec,
                pl.BlockSpec((1, width, length), lambda s, *_: (s, 0, 0)),
                row_spec,
                row_spec,
                row_spec,
                pl.BlockSpec((PITCH * length, LANES), lambda s, *_: (s, 0)),
            ],
            scratch_shapes=[pltpu.VMEM((PITCH * TILE, LANES), F32)] * 3,
        ),
        out_shape=[
            jax.ShapeDtypeStruct((spans, length, 512), BF16),
            jax.ShapeDtypeStruct((spans, width, length), BF16),
            rows_f32,
            rows_f32,
            rows_f32,
            jax.ShapeDtypeStruct((spans * PITCH * length, LANES), F32),
        ],
        compiler_params=params(),
        cost_estimate=cost(0, 300e6),
        name="edges",
    )(src_idx, rel_idx, tgt_idx, live, left4, rel4, right4)


def target_kernel(tgt_idx, live, gt_ref, gr4):
    span = pl.program_id(0)

    @pl.when(span == 0)
    def _():
        gr4[...] = jnp.zeros(gr4.shape, F32)

    def some(n, _):
        r0 = pl.multiple_of(n * GROUP, GROUP)
        for v in range(0, GROUP, 2):
            add_rows(((tgt_idx, gr4, gt_ref),), span, r0 + v, r0, v, 2)
        return 0

    lax.fori_loop(0, tiles_of(live[span]) * (TILE // GROUP), some, 0)


def target_grads(tgt_idx, live, gt, size):
    spans, length = tgt_idx.shape
    return pl.pallas_call(
        target_kernel,
        grid_spec=pltpu.PrefetchScalarGridSpec(
            num_scalar_prefetch=2,
            grid=(spans,),
            in_specs=[pl.BlockSpec((PITCH * length, LANES), lambda s, *_: (s, 0))],
            out_specs=whole((size, LANES)),
        ),
        out_shape=jax.ShapeDtypeStruct((size, LANES), F32),
        compiler_params=params(),
        cost_estimate=cost(0, 100e6),
        name="target_grads",
    )(tgt_idx, live, gt)


def later_span_kernel(live, neg_ref, p_ref, pt_ref, _, *refs, first):
    span_kernel(live, neg_ref, p_ref, pt_ref, *refs, first=first)


def span_kernel(live, neg_ref, p_ref, pt_ref, gp_ref, gn_ref, negs, acc, *, first):
    shards, width, npp = neg_ref.shape
    count = live[first + pl.program_id(0)]
    for o in range(shards):
        negs[:width, o * npp : (o + 1) * npp] = neg_ref[o]
    negs[width:, :] = jnp.zeros((negs.shape[0] - width, shards * npp), BF16)
    acc[...] = jnp.zeros(acc.shape, F32)

    def step(t, _):
        base = pl.multiple_of(t * TILE, TILE)
        here = pl.ds(base, TILE)
        n = negs[...]
        row = lax.broadcasted_iota(jnp.int32, (TILE, 1), 0) + base
        half = jnp.where(row < count, 0.5, 0.0)
        scores = jnp.dot(p_ref[0, here, :], n, preferred_element_type=F32)
        ng = (half * jnp.tanh(0.5 * scores) + half).astype(BF16)
        gp_ref[0, here, :] = lax.dot_general(ng, n, (((1,), (1,)), ((), ())), preferred_element_type=F32)
        acc[...] += jnp.dot(pt_ref[0, :, here], ng, preferred_element_type=F32)
        return 0

    lax.fori_loop(0, tiles_of(count), step, 0)
    for o in range(shards):
        gn_ref[o] = acc[:, o * npp : (o + 1) * npp].astype(BF16)


def span_grads(live, negatives, p, pt, grad_products, first, count):
    shards, width, lanes = negatives.shape
    npp = lanes // count
    spans, length, _ = p.shape
    later = grad_products is not None
    return pl.pallas_call(
        functools.partial(later_span_kernel if later else span_kernel, first=first),
        grid_spec=pltpu.PrefetchScalarGridSpec(
            num_scalar_prefetch=1,
            grid=(count,),
            in_specs=[
                pl.BlockSpec((shards, width, npp), lambda s, *_: (0, 0, s)),
                pl.BlockSpec((1, length, 512), lambda s, *_: (s + first, 0, 0)),
                pl.BlockSpec((1, width, length), lambda s, *_: (s + first, 0, 0)),
            ]
            + ([pl.BlockSpec(memory_space=pl.ANY)] if later else []),
            out_specs=[
                pl.BlockSpec((1, length, 512), lambda s, *_: (s + first, 0, 0)),
                pl.BlockSpec((shards, width, npp), lambda s, *_: (0, 0, s)),
            ],
            scratch_shapes=[
                pltpu.VMEM((512, shards * npp), BF16),
                pltpu.VMEM((width, shards * npp), F32),
            ],
        ),
        out_shape=[
            jax.ShapeDtypeStruct((spans, length, 512), F32),
            jax.ShapeDtypeStruct((shards, width, lanes), BF16),
        ],
        input_output_aliases={4: 0} if later else {},
        compiler_params=params(),
        cost_estimate=cost(count * 6 * length * 512 * shards * npp, 8 * count * length * 512),
        name="span_grads",
    )(live, negatives, p, pt, *([grad_products] if later else []))


def source_kernel(
    src_idx, rel_idx, live, gp_ref, src_ref, rel_ref, tgt_ref, gl_in, gk_in, gl4, gk4, st_s, st_r, *, first
):
    span = pl.program_id(0)

    @pl.when(span == 0)
    def _():
        if gl_in is None:
            gl4[...] = jnp.zeros(gl4.shape, F32)
            gk4[...] = jnp.zeros(gk4.shape, F32)
        else:
            gl4[...] = gl_in[...]
            gk4[...] = gk_in[...]

    def one_tile(tile, _):
        base = pl.multiple_of(tile * TILE, TILE)
        sub = 32
        lane = lax.broadcasted_iota(jnp.int32, (sub, LANES), 1)
        low = lane < 72

        @pl.loop(0, TILE, step=sub)
        def _(r0):
            r0 = pl.multiple_of(r0, sub)
            here = pl.ds(pl.multiple_of(base + r0, sub), sub)
            n, s, r, t = (
                [ref[0, here, j * LANES : (j + 1) * LANES] for j in range(4)]
                for ref in (gp_ref, src_ref, rel_ref, tgt_ref)
            )
            re0 = n[0] + t[0]
            re1 = n[1] + t[1]
            im0 = pltpu.roll(jnp.where(low, n[2], n[1]), 56, 1) + t[2]
            im1 = pltpu.roll(jnp.where(low, n[3], n[2]), 56, 1) + t[3]
            for other, stage in ((r, st_s), (s, st_r)):
                grads = (
                    re0 * other[0] + im0 * other[2],
                    re1 * other[1] + im1 * other[3],
                    im0 * other[0] - re0 * other[2],
                    im1 * other[1] - re1 * other[3],
                )
                for j in range(4):
                    stage[column(r0, j, sub), :] = grads[j]

        @pl.loop(0, TILE, step=GROUP)
        def _(r0):
            for v in range(0, GROUP, 2):
                add_rows(((src_idx, gl4, st_s), (rel_idx, gk4, st_r)), first + span, base + r0 + v, r0, v, 2)

        return 0

    lax.fori_loop(0, tiles_of(live[first + span]), one_tile, 0)


def first_source_kernel(src_idx, rel_idx, live, gp, src, rel, tgt, gl4, gk4, st_s, st_r, *, first):
    source_kernel(src_idx, rel_idx, live, gp, src, rel, tgt, None, None, gl4, gk4, st_s, st_r, first=first)


def source_grads(src_idx, rel_idx, live, gp, src, rel, tgt, totals, sizes, first, count):
    spans, length = src_idx.shape
    row_spec = pl.BlockSpec((1, length, 512), lambda s, *_: (s + first, 0, 0))
    outs = [whole((n, LANES)) for n in sizes]
    body = first_source_kernel if totals is None else source_kernel
    return pl.pallas_call(
        functools.partial(body, first=first),
        grid_spec=pltpu.PrefetchScalarGridSpec(
            num_scalar_prefetch=3,
            grid=(count,),
            in_specs=[row_spec] * 4 + ([] if totals is None else outs),
            out_specs=outs,
            scratch_shapes=[pltpu.VMEM((PITCH * TILE, LANES), F32)] * 2,
        ),
        out_shape=[jax.ShapeDtypeStruct((n, LANES), F32) for n in sizes],
        compiler_params=params(),
        cost_estimate=cost(0, 30e6 * count),
        name="source_grads",
    )(src_idx, rel_idx, live, gp, src, rel, tgt, *(totals or ()))


def joined(ref, b, width):
    return [
        ref[pl.ds(4 * LANES * b + j, LANES, stride=4), :].T[:size]
        for j, (_, size) in enumerate(parts_of(width))
    ]


def rotate_kernel(me, x_ref, o_ref):
    o_ref[...] = x_ref[...]


def rotated(x, me, n):
    block = (x.shape[0] // n, x.shape[1])
    return pl.pallas_call(
        rotate_kernel,
        grid_spec=pltpu.PrefetchScalarGridSpec(
            num_scalar_prefetch=1,
            grid=(n,),
            in_specs=[pl.BlockSpec(block, lambda k, me: (lax.rem(k + me[0], n), 0))],
            out_specs=pl.BlockSpec(block, lambda k, me: (k, 0)),
        ),
        out_shape=jax.ShapeDtypeStruct(x.shape, F32),
        compiler_params=params(),
        cost_estimate=cost(0, 8 * x.size),
        name="rotated",
    )(me.reshape(1).astype(jnp.int32), x)


def summed_blocks(x, axis, held):
    n = lax.axis_size(axis)
    rows = x.shape[0] // n
    total = after(x[:rows], held)
    for k in range(1, n):
        total += lax.ppermute(x[k * rows : (k + 1) * rows], axis, [(i, (i + k) % n) for i in range(n)])
    return total


def relation_kernel(g_ref, t_ref, s_ref, _, o_ref, *, width, rows, spare):
    grads = [g_ref[pl.ds(j, rows, stride=4), :] for j in range(4)]
    square = grads[0] * grads[0] + grads[1] * grads[1] + grads[2] * grads[2] + grads[3] * grads[3]
    state = s_ref[...] + jnp.sum(square, -1, keepdims=True) * (1.0 / width)
    scale = LEARN_RATE / (jnp.sqrt(state) + EPSILON)
    lane = lax.broadcasted_iota(jnp.int32, (rows, LANES), 1)
    for j in range(4):
        new = t_ref[pl.ds(j, rows, stride=4), :] - grads[j] * scale
        if j == 1:
            new = jnp.where(lane == spare, state, new)
        o_ref[pl.ds(j, rows, stride=4), :] = new


def update_relations(g4, t4, state, held, width):
    rows = state.shape[0]
    spare = parts_of(width)[1][1]
    full = [pl.BlockSpec(x.shape, lambda: (0, 0)) for x in (g4, t4, state)]
    return pl.pallas_call(
        functools.partial(relation_kernel, width=width, rows=rows, spare=spare),
        in_specs=full + [pl.BlockSpec(memory_space=pl.ANY)],
        out_specs=full[0],
        out_shape=jax.ShapeDtypeStruct(g4.shape, F32),
        compiler_params=params(),
        cost_estimate=cost(0, 3e6),
        name="update_relations",
    )(g4, t4, state, held)


def join_kernel(g_ref, o_ref, s_ref, *, width, cols):
    spare = parts_of(width)[1][1]
    for b in range(cols // LANES):
        here = slice(b * LANES, min((b + 1) * LANES, o_ref.shape[1]))
        count = here.stop - here.start
        for j, (start, size) in enumerate(parts_of(width)):
            x = g_ref[pl.ds(4 * LANES * b + j, LANES, stride=4), :].T
            o_ref[start : start + size, here] = x[:size, :count]
            if j == 1:
                s_ref[:, here] = x[spare : spare + 1, :count]


def join_relations(rows4, width, kinds):
    return pl.pallas_call(
        functools.partial(join_kernel, width=width, cols=rows4.shape[0] // 4),
        in_specs=[pl.BlockSpec(rows4.shape, lambda: (0, 0))],
        out_specs=[pl.BlockSpec((width, kinds), lambda: (0, 0)), pl.BlockSpec((1, kinds), lambda: (0, 0))],
        out_shape=[jax.ShapeDtypeStruct((width, kinds), F32), jax.ShapeDtypeStruct((1, kinds), F32)],
        compiler_params=params(),
        cost_estimate=cost(0, 4 * kinds * (width + 512)),
        name="join_relations",
    )(rows4)


def update(grad, t_ref, s_ref, q_ref, m_ref, start, size):
    here = slice(start, start + size)
    width = t_ref.shape[0]
    state = s_ref[0:1, here] + jnp.sum(grad * grad, 0, keepdims=True) * (1.0 / width)
    new = t_ref[:, here] - grad * (LEARN_RATE / (jnp.sqrt(state) + EPSILON))
    top = jnp.max(jnp.abs(new), 0, keepdims=True)
    code = new * (CODE / jnp.maximum(top, 1e-30))
    q_ref[:, here] = jnp.round(code).astype(jnp.int32).astype(jnp.int16)
    m_ref[0:1, here] = top
    m_ref[1:2, here] = state


def left_kernel(g_ref, t_ref, s_ref, q_ref, m_ref, *, width, cols):
    for b in range(cols // LANES):
        grad = jnp.concatenate(joined(g_ref, b, width), 0)
        update(grad, t_ref, s_ref, q_ref, m_ref, b * LANES, LANES)


def coded_shapes(width, rows):
    return [jax.ShapeDtypeStruct((width, rows), jnp.int16), jax.ShapeDtypeStruct((2, rows), F32)]


def update_left(g4, table_t, state, cols, start, blocks):
    width, rows = table_t.shape
    return pl.pallas_call(
        functools.partial(left_kernel, width=width, cols=cols),
        grid=(blocks,),
        in_specs=[
            pl.BlockSpec((4 * cols, LANES), lambda i: (i + start, 0)),
            pl.BlockSpec((width, cols), lambda i: (0, i + start)),
            pl.BlockSpec((1, cols), lambda i: (0, i + start)),
        ],
        out_specs=[pl.BlockSpec((width, cols), lambda i: (0, i)), pl.BlockSpec((2, cols), lambda i: (0, i))],
        out_shape=coded_shapes(width, blocks * cols),
        compiler_params=params(),
        cost_estimate=cost(0, 10 * blocks * cols * width),
        name="update_left",
    )(g4, table_t, state)


def negative_sum(acc, idx_ref, b_ref, cols, step, start=0):
    shards, _, lanes = b_ref.shape
    row = lax.broadcasted_iota(jnp.int16, (cols, step), 0)
    one, zero = jnp.ones((), BF16), jnp.zeros((), BF16)
    for q in range(shards):
        for k in range(0, lanes, step):
            idx = (idx_ref[q, :, k : k + step] - (pl.program_id(0) + start) * cols).astype(jnp.int16)
            hot = jnp.where(row == idx, one, zero)
            acc += lax.dot_general(
                b_ref[q, :, k : k + step], hot, (((1,), (1,)), ((), ())), preferred_element_type=F32
            )
    return acc


def first_spread_kernel(idx_ref, b_ref, o_ref, *, cols, step):
    o_ref[...] = negative_sum(jnp.zeros(o_ref.shape, F32), idx_ref, b_ref, cols, step)


def spread_kernel(g_ref, g4_ref, idx_ref, b_ref, o_ref, *, cols, step):
    o_ref[...] = negative_sum(g_ref[...], idx_ref, b_ref, cols, step)
    width = o_ref.shape[0]
    for b in range(cols // LANES):
        for (start, size), x in zip(parts_of(width), joined(g4_ref, b, width)):
            o_ref[start : start + size, b * LANES : (b + 1) * LANES] += x


def spread_update_kernel(g_ref, idx_ref, b_ref, t_ref, s_ref, q_ref, m_ref, acc, *, cols, step, start):
    acc[...] = negative_sum(g_ref[...], idx_ref, b_ref, cols, step, start)
    for b in range(cols // LANES):
        update(acc[:, b * LANES : (b + 1) * LANES], t_ref, s_ref, q_ref, m_ref, b * LANES, LANES)


def spread(grads, idx, returned, rows, cols):
    shards, width, lanes = returned.shape
    block = pl.BlockSpec((width, cols), lambda i: (0, i))
    return pl.pallas_call(
        functools.partial(
            spread_kernel if grads else first_spread_kernel,
            cols=cols, step=2 * LANES if lanes % 256 == 0 else LANES,
        ),
        grid=(rows // cols,),
        in_specs=([block, pl.BlockSpec((4 * cols, LANES), lambda i: (i, 0))] if grads else [])
        + [whole(idx.shape), whole(returned.shape)],
        out_specs=block,
        out_shape=jax.ShapeDtypeStruct((width, rows), F32),
        compiler_params=params(),
        cost_estimate=cost(2 * width * rows * shards * lanes, 8 * width * rows),
        name="spread",
    )(*grads, idx, returned)


def spread_update(grad_t, idx, returned, table_t, state, cols, start, blocks):
    width, rows = grad_t.shape
    shards, _, lanes = returned.shape
    here = pl.BlockSpec((width, cols), lambda i: (0, i + start))
    return pl.pallas_call(
        functools.partial(
            spread_update_kernel, cols=cols, step=2 * LANES if lanes % 256 == 0 else LANES, start=start
        ),
        grid=(blocks,),
        in_specs=[
            here, whole(idx.shape), whole(returned.shape), here, pl.BlockSpec((1, cols), lambda i: (0, i + start)),
        ],
        out_specs=[pl.BlockSpec((width, cols), lambda i: (0, i)), pl.BlockSpec((2, cols), lambda i: (0, i))],
        out_shape=coded_shapes(width, blocks * cols),
        scratch_shapes=[pltpu.VMEM((width, cols), F32)],
        compiler_params=params(),
        cost_estimate=cost(2 * width * blocks * cols * shards * lanes, 8 * width * blocks * cols),
        name="spread_update",
    )(grad_t, idx, returned, table_t, state)


def decode_kernel(m_ref, *refs, ways):
    code = sum(ref[...].astype(jnp.int32) for ref in refs[:ways])
    refs[-1][...] = code.astype(F32) * (m_ref[0:1, :] * (1.0 / CODE))


def decode(codes, meta, rows, cols, start, table_t):
    width, count = codes[0].shape
    ways = len(codes)
    block = pl.BlockSpec((width, cols), lambda i: (0, i))
    return pl.pallas_call(
        functools.partial(decode_kernel, ways=ways),
        grid=(count // cols,),
        in_specs=[pl.BlockSpec((2, cols), lambda i: (0, i))]
        + [block] * ways
        + ([] if table_t is None else [pl.BlockSpec(memory_space=pl.ANY)]),
        out_specs=pl.BlockSpec((width, cols), lambda i: (0, i + start)),
        out_shape=jax.ShapeDtypeStruct((width, rows), F32),
        input_output_aliases={} if table_t is None else {1 + ways: 0},
        compiler_params=params(),
        cost_estimate=cost(0, 6 * width * count),
        name="decode",
    )(meta, *codes, *([] if table_t is None else [table_t]))


def passed_along(block, axis, distance):
    devices = range(lax.axis_size(axis))
    route = [((i - distance) % len(devices), i) for i in devices]
    return lax.ppermute(block, axis, route)


def corner_senders(n):
    return [i for i in range(n) if i % 4 == 1]


def handed_over(halves, held):
    (first, meta_a), (second, meta_b) = halves
    n = lax.axis_size("grp")
    turning = corner_senders(n)
    there = lax.ppermute(first, "grp", [(i, (i + ROUND - 1) % n) for i in turning])
    straight = lax.ppermute(first, "grp", [(i, (i + ROUND) % n) for i in range(n) if i not in turning])
    other = passed_along(second, "grp", ROUND)
    metas = [passed_along(m, "grp", ROUND) for m in (meta_a, meta_b)]
    here = lax.ppermute(
        after(there, *held), "grp", [((i + ROUND - 1) % n, (i + ROUND) % n) for i in turning]
    )
    return ((straight, here), metas[0]), ((other,), metas[1])


def decoded(arrived, rows, cols, held):
    table, start = None, 0
    for codes, meta in arrived:
        table = decode((after(codes[0], *held), *codes[1:]), meta, rows, cols, start, table)
        start += codes[0].shape[1] // cols
    return table, jnp.concatenate([meta[1] for _, meta in arrived])


def exchanged(blocks):
    return lax.all_to_all(blocks, "shard", split_axis=0, concat_axis=0, tiled=True)


def after(value, *others):
    return lax.optimization_barrier((value, *others))[0]


def local(
    left_table,
    right_table,
    left_state,
    right_state,
    relations,
    relation_state,
    source_rows,
    relation_ids,
    target_rows,
    negative_rows,
    span_sizes,
):
    shards = lax.axis_size("shard")
    spans, span_len = source_rows.shape
    neg_per = negative_rows.shape[1] // shards
    npp = round_up(neg_per, LANES)
    rows, width = left_table.shape
    kinds = relations.shape[0]
    kinds_up = round_up(kinds, LANES)
    length = round_up(span_len, TILE)

    left_t, right_t, rel_t = left_table.T, right_table.T, relations.T
    live = span_sizes[0]

    ids = negative_rows.reshape(spans, shards, neg_per)
    ids = jnp.pad(ids, ((0, 0), (0, 0), (0, npp - neg_per)), constant_values=-1)
    asked = lax.all_to_all(ids.transpose(1, 0, 2), "shard", split_axis=0, concat_axis=0, tiled=True)
    asked_lanes = asked.reshape(shards, spans, 1, npp)

    src_idx, rel_idx, tgt_idx = (
        jnp.pad(a, ((0, 0), (0, length - span_len))) for a in (source_rows, relation_ids, target_rows)
    )
    rel_t_up = jnp.pad(rel_t, ((0, 0), (0, kinds_up - kinds)))

    third = -(-spans // 3)
    (c0, c1, c2) = [(a, min(third, spans - a)) for a in range(0, spans, third)]

    served0 = serve(asked_lanes, right_t, *c0)
    fetched0 = exchanged(served0)
    served1 = serve(after(asked_lanes, served0), right_t, *c1)
    served2 = serve(after(asked_lanes, served1), right_t, *c2)
    left4 = split_rows(after(left_t, served2), 512)
    right4 = split_rows(after(right_t, served2), 512)
    rel4 = split_rows(after(rel_t_up, served2), kinds_up)

    fetched1 = exchanged(after(served1, left4, right4, rel4))
    p, pt, src, rel, tgt, gt = edges(
        src_idx, rel_idx, tgt_idx, live, after(left4, fetched0), rel4, right4, width
    )

    fetched2 = exchanged(after(served2, p))
    gp, gn0 = span_grads(live, after(fetched0, fetched1), p, pt, None, *c0)
    gp, gn1 = span_grads(live, fetched1, p, pt, gp, *c1)
    sizes = (4 * rows, 4 * kinds_up)
    sums = functools.partial(source_grads, src_idx, rel_idx, live)
    totals = sums(gp, src, rel, tgt, None, sizes, *c0)

    returned0 = exchanged(after(gn0, totals[1], fetched2))
    gp, gn2 = span_grads(live, fetched2, p, pt, after(gp, totals[1]), *c2)
    gl4, gk4 = sums(gp, src, rel, tgt, totals, sizes, c1[0], c1[1] + c2[1])

    returned1 = exchanged(after(gn1, gk4, returned0))
    rel_rotated = rotated(gk4, lax.axis_index("grp"), lax.axis_size("grp"))
    lanes0, lanes1, lanes2 = (
        asked[:, a : a + n].reshape(shards, 1, n * npp) for a, n in (c0, c1, c2)
    )
    grad_right = spread((), lanes0, after(returned0, rel_rotated), rows, 512)
    blocks = rows // 512
    halves = ((0, blocks // 2), (blocks // 2, blocks - blocks // 2))
    left_in = after(left_t, grad_right)
    coded_left = [tuple(update_left(gl4, left_in, left_state[None], 512, *half)) for half in halves]
    rel_total4 = summed_blocks(rel_rotated, "grp", coded_left[1][1])
    rel_sum4 = lax.psum(rel_total4, "shard")

    returned2 = exchanged(after(gn2, rel_total4, returned1))
    gr4 = target_grads(tgt_idx, live, after(gt, rel_total4, returned1), 4 * rows)
    moved_left = handed_over(coded_left, (gr4,))
    grad_right = spread((grad_right, gr4), lanes1, returned1, rows, 512)
    grad_right = after(grad_right, *moved_left[0][0], *moved_left[1][0])

    coded = []
    for half in halves:
        coded.append(
            tuple(spread_update(grad_right, lanes2, returned2, right_t, right_state[None], 512, *half))
        )
        grad_right = after(grad_right, coded[-1][1])
    new_left, new_left_state = decoded(moved_left, rows, 512, (coded[1][1],))
    moved_right = handed_over(coded, (coded[1][1],))
    new_right, new_right_state = decoded(moved_right, rows, 512, (new_left,))
    slice_rows = kinds_up // lax.axis_size("grp")
    place = lax.axis_index("grp") * slice_rows
    own_rel4 = lax.dynamic_slice(rel4, (4 * place, 0), (4 * slice_rows, LANES))
    own_state = lax.dynamic_slice(
        jnp.pad(relation_state, (0, kinds_up - kinds))[:, None], (place, 0), (slice_rows, 1)
    )
    new_rel4 = update_relations(rel_sum4, own_rel4, own_state, coded[0][1], width)
    new_rel4 = lax.all_gather(new_rel4, "grp", axis=0, tiled=True)
    new_rel_t, new_relation_state = join_relations(new_rel4, width, kinds)
    return (new_left.T, new_left_state, new_right.T, new_right_state, new_rel_t.T, new_relation_state[0])


def solution(mesh):
    rows2, rows1 = P(("grp", "shard"), None), P(("grp", "shard"))
    return jax.shard_map(
        local,
        mesh=mesh,
        in_specs=(rows2, rows2, rows1, rows1, P(), P(), rows2, rows2, rows2, rows2, rows2),
        out_specs=(rows2, rows1, rows2, rows1, P(), P()),
        check_vma=False,
    )
```

time: 1850 us -> 603 us (0.33)
  local copies, waits for them, and re-layouts: 684 us -> 22.2 us
  other arithmetic: 530 us -> 4.38 us
  Pallas kernels: 0 us -> 415 us
  waiting for transfers between devices: 475 us -> 64.2 us
  matrix products: 97.1 us -> 0 us
  starting transfers between devices: 26.2 us -> 70.4 us
    pallas_call x0 -> x26, Pallas kernels: none -> 415 us  [the longest x2 85.6 us: source_grads(): pl.pallas_call(functools.partial(body, first=first), grid_spec=pltpu.Pref...]
    scatter-add x28 -> x0, other arithmetic: 384 us -> none  [the longest x9 124 us: step(): grad_right = grad_right.at[targets].add(grad_target)]
    gather x38 -> x0, local copies, waits for them, and re-layouts: 285 us -> none  [the longest x18 103 us: step(): target = right_table[targets]]
    all_to_all x3 -> x6, waiting for transfers between devices: 284 us -> 2.88 us  [exchanged(): lax.all_to_all(blocks, 'shard', split_axis=0, concat_axis=0, tiled=True)]
    psum x1, waiting for transfers between devices: 117 us -> 7.52 us  [local(): rel_sum4 = lax.psum(rel_total4, 'shard')]
    dot_general x27 -> x0, matrix products: 97.1 us -> none  [the longest x9 35.6 us: span_terms(): lax.dot_general(neg_grad, product_b, (((0,), (0,)), ((), ())), preferred_...]
    while x199 -> x0, local copies, waits for them, and re-layouts: 91.5 us -> none
    slice x18 -> x6, local copies, waits for them, and re-layouts: 60.1 us -> 3.28 us  [the longest x1 3.22 us: summed_blocks(): x[k * rows:(k + 1) * rows]]
  transfers between devices with their start and end apart: 8 -> 27, of which waited for: 4 -> 7; matrix products, arithmetic and copies ran while one was open for 9% -> 3% of each run, Pallas kernels for 0% -> 65%
where the time goes in v1:
time: 603 us; the launch traced here: 600 us
  Pallas kernels  415 us (69%)
  starting transfers between devices  70.4 us (12%)
  waiting for transfers between devices  64.2 us (11%)
  local copies, waits for them, and re-layouts  22.2 us (4%)
  between operations  14.4 us (2%)
  blocking collectives  9.82 us (2%)
    pallas_call x2, Pallas kernels, source_grads(): pl.pallas_call(functools.partial(body, first=first), grid_spec=pltpu.Pref...  85.6 us
    pallas_call x1, Pallas kernels, edges(): pl.pallas_call(edge_kernel, grid_spec=pltpu.PrefetchScalarGridSpec(num_sc...  83.1 us
    pallas_call x3, Pallas kernels, serve(): pl.pallas_call(functools.partial(serve_kernel, rows=rows, step=512), grid...  49.5 us
    pallas_call x3, Pallas kernels, span_grads(): pl.pallas_call(functools.partial(later_span_kernel if later else span_ker...  44.3 us
    pallas_call x1, Pallas kernels, target_grads(): pl.pallas_call(target_kernel, grid_spec=pltpu.PrefetchScalarGridSpec(num_...  37 us
    all_to_all x6, starting transfers between devices, exchanged(): lax.all_to_all(blocks, 'shard', split_axis=0, concat_axis=0, tiled=True)  33 us
    pallas_call x2, Pallas kernels, spread(): pl.pallas_call(functools.partial(spread_kernel if grads else first_spread...  30.6 us
    ppermute x6, waiting for transfers between devices, passed_along(): return lax.ppermute(block, axis, route)  26.3 us
  transfers between devices with their start and end apart: 27, of which 7 were waited for; matrix products, arithmetic and copies ran while one was open for 3% of the time, Pallas kernels for 65%

profile of v1, /device:TPU:1, one launch (start us, length us, event | category | flops | bytes accessed | tf_op | source)
XLA Modules:
  0.0 600.5 jit_solution(6899142026716289504)
XLA Ops:
  8.1 9.8 %all_to_all.35 = s32[4,9,256]{2,1,0:T(8,128)S(1)} all-to-all(s32[4,9,256]{2,1,0:T(8,128)S(1)} %copy.29), channel_id=1, replica_groups=mesh['grp'=8,'shard'=4] {'shard'}, dimensions={0} | all-to-all | bytes 73728 | tf_op jit(solution)/shard_map/all_to_all | solution.py:705
  18.6 16.5 %serve.3 = bf16[4,400,768]{2,1,0:T(8,128)(2,1)} custom-call(s32[4,9,1,256]{3,2,1,0:T(1,128)} %copy.31.idx_ref, f32[400,4096]{1,0:T(8,128)} %bitcast.25), custom_call_target="tpu_custom_call" | custom-call | flops 10066329600 | bytes 6553600 | tf_op jit(solution)/shard_map/serve/pallas_call | solution.py:88
  35.1 3.6 all-to-all-start.1
  38.8 3.2 pad.26.t_ref
  42.6 16.5 %serve.4 = bf16[4,400,768]{2,1,0:T(8,128)(2,1)} custom-call(s32[4,9,1,256]{3,2,1,0:T(1,128)} %copy.32.idx_ref, f32[400,4096]{1,0:T(8,128)} %bitcast.26), custom_call_target="tpu_custom_call" | custom-call | flops 10066329600 | bytes 6553600 | tf_op jit(solution)/shard_map/serve/pallas_call | solution.py:88
  59.7 16.5 %serve.5 = bf16[4,400,768]{2,1,0:T(8,128)(2,1)} custom-call(s32[4,9,1,256]{3,2,1,0:T(1,128)} %copy.33.idx_ref, f32[400,4096]{1,0:T(8,128)} %bitcast.27), custom_call_target="tpu_custom_call" | custom-call | flops 10066329600 | bytes 6553600 | tf_op jit(solution)/shard_map/serve/pallas_call | solution.py:88
  76.2 4.0 split_rows.4.rel4
  80.3 9.3 %split_rows.3.left4 = f32[16384,128]{1,0:T(8,128)} custom-call(f32[400,4096]{1,0:T(8,128)} %bitcast.20), custom_call_target="tpu_custom_call" | custom-call | bytes 14942208 | tf_op jit(solution)/shard_map/split_rows/pallas_call | solution.py:56
  89.5 9.3 %split_rows.5.right4 = f32[16384,128]{1,0:T(8,128)} custom-call(f32[400,4096]{1,0:T(8,128)} %bitcast.28), custom_call_target="tpu_custom_call" | custom-call | bytes 14942208 | tf_op jit(solution)/shard_map/split_rows/pallas_call | solution.py:56
  100.3 4.5 all-to-all-start.3
  106.7 83.1 %edges.1 = (bf16[9,1024,512]{2,1,0:T(8,128)(2,1)}, bf16[9,400,1024]{2,1,0:T(8,128)(2,1)}, f32[9,1024,512]{2,1,0:T(8,128)}, f32[9,1024,512]{2,1,0:T(8,128)}, f32[...) custom-call(s32[9,1024]{1,0:T(8,128)} %pad.22.src_idx, s32[9,1024]{1,0:T(8,128)} %pad.23.rel_idx, s32[9,1024]{1,0:T(8,128)} %pad.25.tgt_idx, ...), custom_call_target="tpu_custom_call" | custom-call | bytes 300000000 | tf_op jit(solution)/shard_map/edges/pallas_call | solution.py:208
  189.8 4.5 all-to-all-start.2
  194.4 13.4 %span_grads.3 = (f32[9,1024,512]{2,1,0:T(8,128)}, bf16[4,400,768]{2,1,0:T(8,128)(2,1)}) custom-call(s32[9]{0:T(128)} %bitcast.42, bf16[4,400,768]{2,1,0:T(8,128)(2,1)} %copy-done.3, bf16[9,1024,512]{2,1,0:T(8,128)(2,1)} %get-tuple-element.63.p_ref, bf16[9,400,1024]{2,1,0:T(8,128)(2,1)} %get-tuple-element.65.pt_ref), custom_call_target="tpu_custom_call" | custom-call | flops 9663676416 | bytes 12582912 | tf_op jit(solution)/shard_map/span_grads/pallas_call | solution.py:305
  207.7 16.2 %span_grads.4 = (f32[9,1024,512]{2,1,0:T(8,128)}, bf16[4,400,768]{2,1,0:T(8,128)(2,1)}) custom-call(s32[9]{0:T(128)} %bitcast.43, bf16[4,400,768]{2,1,0:T(8,128)(2,1)} %copy-done, bf16[9,1024,512]{2,1,0:T(8,128)(2,1)} %get-tuple-element.63.p_ref, bf16[9,400,1024]{2,1,0:T(8,128)(2,1)} %get-tuple-element.65.pt_ref, ...), custom_call_target="tpu_custom_call", output_to_operand_aliasing={{0}: (4, {})} | custom-call | flops 9663676416 | bytes 12582912 | tf_op jit(solution)/shard_map/span_grads/pallas_call | solution.py:305
  223.9 28.6 %source_grads.2 = (f32[16384,128]{1,0:T(8,128)}, f32[5632,128]{1,0:T(8,128)}) custom-call(s32[9,1024]{1,0:T(8,128)} %pad.22.src_idx, s32[9,1024]{1,0:T(8,128)} %pad.23.rel_idx, s32[9]{0:T(128)} %bitcast.44, f32[9,1024,512]{2,1,0:T(8,128)} %get-tuple-element.74.gp._, f32[9,1024,512]{2,1,0:T(8,128)} %get-tuple-element.70.src.src_ref, ...), custom_call_target="tpu_custom_call" | custom-call | bytes 90000000 | tf_op jit(solution)/shard_map/source_grads/pallas_call | solution.py:397
  252.5 8.8 %all-to-all-start.4 = ((bf16[4,400,768]{2,1,0:T(8,128)(2,1)}), bf16[4,400,768]{2,1,0:T(8,128)(2,1)S(1)}, u32[]{:S(2)}, u32[]{:S(2)}) async-start(bf16[4,400,768]{2,1,0:T(8,128)(2,1)} %get-tuple-element.79), calls=%async_computation.4 | async-start | bytes 4915200 | tf_op jit(solution)/shard_map/all_to_all | solution.py:671
  261.3 14.8 %span_grads.5 = (f32[9,1024,512]{2,1,0:T(8,128)}, bf16[4,400,768]{2,1,0:T(8,128)(2,1)}) custom-call(s32[9]{0:T(128)} %bitcast.45, bf16[4,400,768]{2,1,0:T(8,128)(2,1)} %all-to-all-done.2.neg_ref, bf16[9,1024,512]{2,1,0:T(8,128)(2,1)} %get-tuple-element.63.p_ref, bf16[9,400,1024]{2,1,0:T(8,128)(2,1)} %get-tuple-element.65.pt_ref, ...), custom_call_target="tpu_custom_call", output_to_operand_aliasing={{0}: (4, {})} | custom-call | flops 9663676416 | bytes 12582912 | tf_op jit(solution)/shard_map/span_grads/pallas_call | solution.py:305
  276.1 57.0 %source_grads.3 = (f32[16384,128]{1,0:T(8,128)}, f32[5632,128]{1,0:T(8,128)}) custom-call(s32[9,1024]{1,0:T(8,128)} %pad.22.src_idx, s32[9,1024]{1,0:T(8,128)} %pad.23.rel_idx, s32[9]{0:T(128)} %bitcast.46, f32[9,1024,512]{2,1,0:T(8,128)} %get-tuple-element.75.gp_ref, f32[9,1024,512]{2,1,0:T(8,128)} %get-tuple-element.70.src.src_ref, ...), custom_call_target="tpu_custom_call" | custom-call | bytes 180000000 | tf_op jit(solution)/shard_map/source_grads/pallas_call | solution.py:397
  334.5 6.9 %all-to-all-start.5 = ((bf16[4,400,768]{2,1,0:T(8,128)(2,1)}), bf16[4,400,768]{2,1,0:T(8,128)(2,1)S(1)}, u32[]{:S(2)}, u32[]{:S(2)}) async-start(bf16[4,400,768]{2,1,0:T(8,128)(2,1)} %get-tuple-element.88), calls=%async_computation.5 | async-start | bytes 4915200 | tf_op jit(solution)/shard_map/all_to_all | solution.py:671
  341.5 6.0 rotated.1
  347.5 3.2 fusion
  350.7 4.1 collective-permute-start.2
  355.4 3.5 collective-permute-start.7
  362.5 3.2 collective-permute-done.8
  365.7 3.1 collective-permute-start.3
  368.9 14.4 %spread.2.g_ref = f32[400,4096]{1,0:T(8,128)} custom-call(s32[4,1,768]{2,1,0:T(1,128)} %reshape.37.idx_ref, bf16[4,400,768]{2,1,0:T(8,128)(2,1)} %copy-done.2), custom_call_target="tpu_custom_call" | custom-call | flops 10066329600 | bytes 13107200 | tf_op jit(solution)/shard_map/spread/pallas_call | solution.py:577
  383.3 5.7 update_left.2
  390.9 2.9 all-to-all-done.5.b_ref
  393.8 4.5 all-to-all-start.6
  398.4 5.8 update_left.3
  404.2 1.9 collective-permute-start.10
  407.4 6.1 %collective-permute-start.1 = (s16[400,2048]{1,0:T(8,128)(2,1)}, s16[400,2048]{1,0:T(8,128)(2,1)}, u32[]{:S(2)}, u32[]{:S(2)}) collective-permute-start(s16[400,2048]{1,0:T(8,128)(2,1)} %get-tuple-element.84), channel_id=1, source_target_pairs={{12,0},{16,4},{20,8},{24,12},{28,16},{0,20},{4,24},{8,28},{13,1},{... | collective-permute-start | bytes 4915208 | tf_op jit(solution)/shard_map/ppermute | solution.py:641
  413.5 37.0 %target_grads.1.g4_ref = f32[16384,128]{1,0:T(8,128)} custom-call(s32[9,1024]{1,0:T(8,128)} %pad.25.tgt_idx, s32[9]{0:T(128)} %bitcast.47, f32[46080,128]{1,0:T(8,128)} %get-tuple-element.89.gt_ref), custom_call_target="tpu_custom_call" | custom-call | bytes 100000000 | tf_op jit(solution)/shard_map/target_grads/pallas_call | solution.py:256
  455.8 16.2 %spread.3.g_ref = f32[400,4096]{1,0:T(8,128)} custom-call(f32[400,4096]{1,0:T(8,128)} %spread.2.g_ref, f32[16384,128]{1,0:T(8,128)} %target_grads.1.g4_ref, s32[4,1,768]{2,1,0:T(1,128)} %reshape.38.idx_ref, bf16[4,400,768]{2,1,0:T(8,128)(2,1)} %copy-done.1), custom_call_target="tpu_custom_call" | custom-call | flops 10066329600 | bytes 13107200 | tf_op jit(solution)/shard_map/spread/pallas_call | solution.py:577
  472.0 11.5 %spread_update.2 = (s16[400,2048]{1,0:T(8,128)(2,1)}, f32[2,2048]{1,0:T(2,128)}) custom-call(f32[400,4096]{1,0:T(8,128)} %spread.3.g_ref, s32[4,1,768]{2,1,0:T(1,128)} %reshape.39.idx_ref, bf16[4,400,768]{2,1,0:T(8,128)(2,1)} %all-to-all-done.6.b_ref, f32[400,4096]{1,0:T(8,128)} %bitcast.29, f32[1,4096]{1,0:T(1,128)} %bitcast.50), custom_call_target="tpu_custom_call" | custom-call | flops 5033164800 | bytes 6553600 | tf_op jit(solution)/shard_map/spread_update/pallas_call | solution.py:597
  483.5 7.5 %all-reduce.8.cloned.1.call-done.g_ref = f32[704,128]{1,0:T(8,128)} async-done(((f32[704,128]{1,0:T(8,128)}), f32[704,128]{1,0:T(8,128)}) %all-reduce.8.cloned.1.call-update) | async-done | bytes 360464 | tf_op jit(solution)/shard_map/psum | solution.py:751
  491.0 2.1 update_relations.1
  493.2 3.2 collective-permute-start.17
  497.8 10.4 %spread_update.3 = (s16[400,2048]{1,0:T(8,128)(2,1)}, f32[2,2048]{1,0:T(2,128)}) custom-call(f32[400,4096]{1,0:T(8,128)} %spread.3.g_ref, s32[4,1,768]{2,1,0:T(1,128)} %reshape.39.idx_ref, bf16[4,400,768]{2,1,0:T(8,128)(2,1)} %all-to-all-done.6.b_ref, f32[400,4096]{1,0:T(8,128)} %bitcast.30, f32[1,4096]{1,0:T(1,128)} %bitcast.51), custom_call_target="tpu_custom_call" | custom-call | flops 5033164800 | bytes 6553600 | tf_op jit(solution)/shard_map/spread_update/pallas_call | solution.py:597
  508.2 1.9 collective-permute-start.14
  510.1 23.3 %collective-permute-done.17 = s16[400,2048]{1,0:T(8,128)(2,1)S(1)} collective-permute-done((s16[400,2048]{1,0:T(8,128)(2,1)}, s16[400,2048]{1,0:T(8,128)(2,1)S(1)}, u32[]{:S(2)}, u32[]{:S(2)}) %collective-permute-start.17) | collective-permute-done | bytes 1638432 | tf_op jit(solution)/shard_map/ppermute | solution.py:652
  536.2 26.1 %collective-permute-done.12.m_ref = f32[2,2048]{1,0:T(2,128)S(1)} collective-permute-done((f32[2,2048]{1,0:T(2,128)S(1)}, f32[2,2048]{1,0:T(2,128)S(1)}, u32[]{:S(2)}, u32[]{:S(2)}) %collective-permute-start.12) | collective-permute-done | bytes 16416 | tf_op jit(solution)/shard_map/ppermute | solution.py:641
  562.5 3.4 collective-permute-start.13
  568.4 4.4 decode.4.refs_1_
  572.8 4.0 decode.5
  579.9 4.4 decode.6.refs_1_
  584.3 4.0 decode.7
  588.3 4.0 join_relations.1
  (104 shorter events, 31.6 us)
Async XLA Ops:
  35.1 63.8 %all-to-all-start.1 = ((bf16[4,400,768]{2,1,0:T(8,128)(2,1)}), bf16[4,400,768]{2,1,0:T(8,128)(2,1)S(1)}, u32[]{:S(2)}, u32[]{:S(2)}) async-start(bf16[4,400,768]{2,1,0:T(8,128)(2,1)} %serve.3), calls=%async_computation.1 | async-start | bytes 4915200 | tf_op jit(solution)/shard_map/all_to_all | solution.py:671
  98.9 5.9 copy-start.9
  98.9 6.6 %copy-start.10 = (s32[9,1000]{1,0:T(8,128)S(1)}, s32[9,1000]{1,0:T(8,128)}, u32[]{:S(2)}) copy-start(s32[9,1000]{1,0:T(8,128)} %param.18) | copy-start | bytes 108004
  98.9 7.2 %copy-start.11 = (s32[9,1000]{1,0:T(8,128)S(1)}, s32[9,1000]{1,0:T(8,128)}, u32[]{:S(2)}) copy-start(s32[9,1000]{1,0:T(8,128)} %param.19) | copy-start | bytes 108004
  98.9 1.4 copy-start.3
  100.3 89.5 %all-to-all-start.3 = ((bf16[4,400,768]{2,1,0:T(8,128)(2,1)}), bf16[4,400,768]{2,1,0:T(8,128)(2,1)S(1)}, u32[]{:S(2)}, u32[]{:S(2)}) async-start(bf16[4,400,768]{2,1,0:T(8,128)(2,1)} %serve.4), calls=%async_computation.3 | async-start | bytes 4915200 | tf_op jit(solution)/shard_map/all_to_all | solution.py:671
  189.8 17.9 %copy-start = (bf16[4,400,768]{2,1,0:T(8,128)(2,1)}, bf16[4,400,768]{2,1,0:T(8,128)(2,1)S(1)}, u32[]{:S(2)}) copy-start(bf16[4,400,768]{2,1,0:T(8,128)(2,1)S(1)} %all-to-all-done.3.neg_ref) | copy-start | bytes 7372804
  189.8 62.6 %all-to-all-start.2 = ((bf16[4,400,768]{2,1,0:T(8,128)(2,1)}), bf16[4,400,768]{2,1,0:T(8,128)(2,1)}, u32[]{:S(2)}, u32[]{:S(2)}) async-start(bf16[4,400,768]{2,1,0:T(8,128)(2,1)} %serve.5), calls=%async_computation.2 | async-start | bytes 4915200 | tf_op jit(solution)/shard_map/all_to_all | solution.py:671
  252.5 80.6 %all-to-all-start.4 = ((bf16[4,400,768]{2,1,0:T(8,128)(2,1)}), bf16[4,400,768]{2,1,0:T(8,128)(2,1)S(1)}, u32[]{:S(2)}, u32[]{:S(2)}) async-start(bf16[4,400,768]{2,1,0:T(8,128)(2,1)} %get-tuple-element.79), calls=%async_computation.4 | async-start | bytes 4915200 | tf_op jit(solution)/shard_map/all_to_all | solution.py:671
  333.1 1.4 copy-start.2
  334.5 59.3 %all-to-all-start.5 = ((bf16[4,400,768]{2,1,0:T(8,128)(2,1)}), bf16[4,400,768]{2,1,0:T(8,128)(2,1)S(1)}, u32[]{:S(2)}, u32[]{:S(2)}) async-start(bf16[4,400,768]{2,1,0:T(8,128)(2,1)} %get-tuple-element.88), calls=%async_computation.5 | async-start | bytes 4915200 | tf_op jit(solution)/shard_map/all_to_all | solution.py:671
  350.7 10.8 %collective-permute-start.2 = (f32[704,128]{1,0:T(8,128)}, f32[704,128]{1,0:T(8,128)S(1)}, u32[]{:S(2)}, u32[]{:S(2)}) collective-permute-start(f32[704,128]{1,0:T(8,128)} %get-tuple-element.108), channel_id=1, source_target_pairs={{0,4},{4,8},{8,12},{12,16},{16,20},{20,24},{24,28},{28,0},{1,5},{5... | collective-permute-start | bytes 1081352 | tf_op jit(solution)/shard_map/ppermute | solution.py:446
  354.8 11.0 %collective-permute-start.8 = (f32[704,128]{1,0:T(8,128)}, f32[704,128]{1,0:T(8,128)}, u32[]{:S(2)}, u32[]{:S(2)}) collective-permute-start(f32[704,128]{1,0:T(8,128)} %get-tuple-element.109), channel_id=1, source_target_pairs={{0,28},{4,0},{8,4},{12,8},{16,12},{20,16},{24,20},{28,24},{1,29},{... | collective-permute-start | bytes 1081352 | tf_op jit(solution)/shard_map/ppermute | solution.py:446
  355.4 33.7 %collective-permute-start.7 = (f32[704,128]{1,0:T(8,128)}, f32[704,128]{1,0:T(8,128)S(1)}, u32[]{:S(2)}, u32[]{:S(2)}) collective-permute-start(f32[704,128]{1,0:T(8,128)} %get-tuple-element.110), channel_id=1, source_target_pairs={{0,24},{4,28},{8,0},{12,4},{16,8},{20,12},{24,16},{28,20},{1,25},{... | collective-permute-start | bytes 1081352 | tf_op jit(solution)/shard_map/ppermute | solution.py:446
  358.9 30.2 %collective-permute-start.6 = (f32[704,128]{1,0:T(8,128)}, f32[704,128]{1,0:T(8,128)S(1)}, u32[]{:S(2)}, u32[]{:S(2)}) collective-permute-start(f32[704,128]{1,0:T(8,128)} %get-tuple-element.111), channel_id=1, source_target_pairs={{0,20},{4,24},{8,28},{12,0},{16,4},{20,8},{24,12},{28,16},{1,21},{... | collective-permute-start | bytes 1081352 | tf_op jit(solution)/shard_map/ppermute | solution.py:446
  360.5 28.5 %collective-permute-start.5 = (f32[704,128]{1,0:T(8,128)}, f32[704,128]{1,0:T(8,128)S(1)}, u32[]{:S(2)}, u32[]{:S(2)}) collective-permute-start(f32[704,128]{1,0:T(8,128)} %get-tuple-element.112), channel_id=1, source_target_pairs={{0,16},{4,20},{8,24},{12,28},{16,0},{20,4},{24,8},{28,12},{1,17},{... | collective-permute-start | bytes 1081352 | tf_op jit(solution)/shard_map/ppermute | solution.py:446
  361.4 27.6 %collective-permute-start.4 = (f32[704,128]{1,0:T(8,128)}, f32[704,128]{1,0:T(8,128)S(1)}, u32[]{:S(2)}, u32[]{:S(2)}) collective-permute-start(f32[704,128]{1,0:T(8,128)} %get-tuple-element.113), channel_id=1, source_target_pairs={{0,12},{4,16},{8,20},{12,24},{16,28},{20,0},{24,4},{28,8},{1,13},{... | collective-permute-start | bytes 1081352 | tf_op jit(solution)/shard_map/ppermute | solution.py:446
  365.7 23.4 %collective-permute-start.3 = (f32[704,128]{1,0:T(8,128)}, f32[704,128]{1,0:T(8,128)S(1)}, u32[]{:S(2)}, u32[]{:S(2)}) collective-permute-start(f32[704,128]{1,0:T(8,128)} %get-tuple-element.114), channel_id=1, source_target_pairs={{0,8},{4,12},{8,16},{12,20},{16,24},{20,28},{24,0},{28,4},{1,9},{5... | collective-permute-start | bytes 1081352 | tf_op jit(solution)/shard_map/ppermute | solution.py:446
  393.8 10.4 %copy-start.1 = (bf16[4,400,768]{2,1,0:T(8,128)(2,1)}, bf16[4,400,768]{2,1,0:T(8,128)(2,1)S(1)}, u32[]{:S(2)}) copy-start(bf16[4,400,768]{2,1,0:T(8,128)(2,1)S(1)} %all-to-all-done.5.b_ref) | copy-start | bytes 7372804
  393.8 78.2 %all-to-all-start.6 = ((bf16[4,400,768]{2,1,0:T(8,128)(2,1)}), bf16[4,400,768]{2,1,0:T(8,128)(2,1)}, u32[]{:S(2)}, u32[]{:S(2)}) async-start(bf16[4,400,768]{2,1,0:T(8,128)(2,1)} %get-tuple-element.94), calls=%async_computation.6 | async-start | bytes 4915200 | tf_op jit(solution)/shard_map/all_to_all | solution.py:671
  398.4 92.7 %all-reduce.8.cloned.1.call-start = ((), (), s32[]{:S(2)}) async-start(), calls=%async_computation.7 | async-start | bytes 720896 | tf_op jit(solution)/shard_map/psum | solution.py:751
  404.2 46.3 %collective-permute-start.10 = (s16[400,2048]{1,0:T(8,128)(2,1)}, s16[400,2048]{1,0:T(8,128)(2,1)}, u32[]{:S(2)}, u32[]{:S(2)}) collective-permute-start(s16[400,2048]{1,0:T(8,128)(2,1)} %get-tuple-element.90), channel_id=1, source_target_pairs={{4,20},{20,4},{5,21},{21,5},{6,22},{22,6},{7,23},{23,7}} | collective-permute-start | bytes 4915208 | tf_op jit(solution)/shard_map/ppermute | solution.py:652
  406.1 65.9 %collective-permute-start.9 = (s16[400,2048]{1,0:T(8,128)(2,1)}, s16[400,2048]{1,0:T(8,128)(2,1)S(1)}, u32[]{:S(2)}, u32[]{:S(2)}) collective-permute-start(s16[400,2048]{1,0:T(8,128)(2,1)} %get-tuple-element.90), channel_id=1, source_target_pairs={{0,20},{8,28},{12,0},{16,4},{24,12},{28,16},{1,21},{9,29},{13,1},{... | collective-permute-start | bytes 4915208 | tf_op jit(solution)/shard_map/ppermute | solution.py:653
  407.4 64.6 %collective-permute-start.1 = (s16[400,2048]{1,0:T(8,128)(2,1)}, s16[400,2048]{1,0:T(8,128)(2,1)}, u32[]{:S(2)}, u32[]{:S(2)}) collective-permute-start(s16[400,2048]{1,0:T(8,128)(2,1)} %get-tuple-element.84), channel_id=1, source_target_pairs={{12,0},{16,4},{20,8},{24,12},{28,16},{0,20},{4,24},{8,28},{13,1},{... | collective-permute-start | bytes 4915208 | tf_op jit(solution)/shard_map/ppermute | solution.py:641
  413.5 38.4 %copy-start.17 = (f32[1345]{0:T(1024)S(1)}, f32[1345]{0:T(1024)}, u32[]{:S(2)}) copy-start(f32[1345]{0:T(1024)} %param.16) | copy-start | bytes 16144
  450.5 21.5 %collective-permute-start.11 = (s16[400,2048]{1,0:T(8,128)(2,1)}, s16[400,2048]{1,0:T(8,128)(2,1)S(1)}, u32[]{:S(2)}, u32[]{:S(2)}) collective-permute-start(s16[400,2048]{1,0:T(8,128)(2,1)} %collective-permute-done.10), channel_id=1, source_target_pairs={{20,24},{4,8},{21,25},{5,9},{22,26},{6,10},{23,27},{7,11}} | collective-permute-start | bytes 4915208 | tf_op jit(solution)/shard_map/ppermute | solution.py:656
  455.8 132.6 %all-gather.2.cloned.1.call-start = ((), (), s32[]{:S(2)}) async-start(), calls=%async_computation.8 | async-start | bytes 3244032 | tf_op jit(solution)/shard_map/all_gather | solution.py:775
  472.0 11.5 %copy-start.4 = (s16[400,2048]{1,0:T(8,128)(2,1)}, s16[400,2048]{1,0:T(8,128)(2,1)S(1)}, u32[]{:S(2)}) copy-start(s16[400,2048]{1,0:T(8,128)(2,1)S(1)} %collective-permute-done.9.refs_0_) | copy-start | bytes 4915204
  472.0 11.5 %copy-start.5 = (s16[400,2048]{1,0:T(8,128)(2,1)}, s16[400,2048]{1,0:T(8,128)(2,1)S(1)}, u32[]{:S(2)}) copy-start(s16[400,2048]{1,0:T(8,128)(2,1)S(1)} %collective-permute-done.11.refs_1_) | copy-start | bytes 4915204
  493.2 42.8 %copy-start.20 = (f32[2,2048]{1,0:T(2,128)S(1)}, f32[2,2048]{1,0:T(2,128)}, u32[]{:S(2)}) copy-start(f32[2,2048]{1,0:T(2,128)} %get-tuple-element.99) | copy-start | bytes 49156
  493.2 42.9 %copy-start.19 = (f32[2,2048]{1,0:T(2,128)S(1)}, f32[2,2048]{1,0:T(2,128)}, u32[]{:S(2)}) copy-start(f32[2,2048]{1,0:T(2,128)} %get-tuple-element.83) | copy-start | bytes 49156
  493.2 72.7 %copy-start.16 = (f32[2,2048]{1,0:T(2,128)S(1)}, f32[2,2048]{1,0:T(2,128)}, u32[]{:S(2)}) copy-start(f32[2,2048]{1,0:T(2,128)} %get-tuple-element.95._) | copy-start | bytes 49156
  493.2 40.2 %collective-permute-start.17 = (s16[400,2048]{1,0:T(8,128)(2,1)}, s16[400,2048]{1,0:T(8,128)(2,1)S(1)}, u32[]{:S(2)}, u32[]{:S(2)}) collective-permute-start(s16[400,2048]{1,0:T(8,128)(2,1)} %get-tuple-element.103), channel_id=1, source_target_pairs={{4,20},{20,4},{5,21},{21,5},{6,22},{22,6},{7,23},{23,7}} | collective-permute-start | bytes 4915208 | tf_op jit(solution)/shard_map/ppermute | solution.py:652
  496.5 81.0 %collective-permute-start.16 = (s16[400,2048]{1,0:T(8,128)(2,1)}, s16[400,2048]{1,0:T(8,128)(2,1)S(1)}, u32[]{:S(2)}, u32[]{:S(2)}) collective-permute-start(s16[400,2048]{1,0:T(8,128)(2,1)} %get-tuple-element.103), channel_id=1, source_target_pairs={{0,20},{8,28},{12,0},{16,4},{24,12},{28,16},{1,21},{9,29},{13,1},{... | collective-permute-start | bytes 4915208 | tf_op jit(solution)/shard_map/ppermute | solution.py:653
  508.2 69.3 %collective-permute-start.14 = (s16[400,2048]{1,0:T(8,128)(2,1)}, s16[400,2048]{1,0:T(8,128)(2,1)S(1)}, u32[]{:S(2)}, u32[]{:S(2)}) collective-permute-start(s16[400,2048]{1,0:T(8,128)(2,1)} %get-tuple-element.101), channel_id=1, source_target_pairs={{12,0},{16,4},{20,8},{24,12},{28,16},{0,20},{4,24},{8,28},{13,1},{... | collective-permute-start | bytes 4915208 | tf_op jit(solution)/shard_map/ppermute | solution.py:641
  533.4 1.2 copy-start.18
  534.6 42.9 %collective-permute-start.18 = (s16[400,2048]{1,0:T(8,128)(2,1)}, s16[400,2048]{1,0:T(8,128)(2,1)S(1)}, u32[]{:S(2)}, u32[]{:S(2)}) collective-permute-start(s16[400,2048]{1,0:T(8,128)(2,1)} %copy-done.18), channel_id=1, source_target_pairs={{20,24},{4,8},{21,25},{5,9},{22,26},{6,10},{23,27},{7,11}} | collective-permute-start | bytes 4915208 | tf_op jit(solution)/shard_map/ppermute | solution.py:656
  536.0 26.3 %collective-permute-start.12 = (f32[2,2048]{1,0:T(2,128)S(1)}, f32[2,2048]{1,0:T(2,128)S(1)}, u32[]{:S(2)}, u32[]{:S(2)}) collective-permute-start(f32[2,2048]{1,0:T(2,128)S(1)} %copy-done.20), channel_id=1, source_target_pairs={{12,0},{16,4},{20,8},{24,12},{28,16},{0,20},{4,24},{8,28},{13,1},{... | collective-permute-start | bytes 49160 | tf_op jit(solution)/shard_map/ppermute | solution.py:641
  536.1 26.4 %collective-permute-start = (f32[2,2048]{1,0:T(2,128)S(1)}, f32[2,2048]{1,0:T(2,128)S(1)}, u32[]{:S(2)}, u32[]{:S(2)}) collective-permute-start(f32[2,2048]{1,0:T(2,128)S(1)} %copy-done.19), channel_id=1, source_target_pairs={{12,0},{16,4},{20,8},{24,12},{28,16},{0,20},{4,24},{8,28},{13,1},{... | collective-permute-start | bytes 49160 | tf_op jit(solution)/shard_map/ppermute | solution.py:641
  562.3 6.1 %copy-start.13 = (f32[2,2048]{1,0:T(2,128)}, f32[2,2048]{1,0:T(2,128)S(1)}, u32[]{:S(2)}) copy-start(f32[2,2048]{1,0:T(2,128)S(1)} %collective-permute-done.12.m_ref) | copy-start | bytes 49156
  562.5 10.3 %copy-start.15 = (f32[2,2048]{1,0:T(2,128)}, f32[2,2048]{1,0:T(2,128)S(1)}, u32[]{:S(2)}) copy-start(f32[2,2048]{1,0:T(2,128)S(1)} %collective-permute-done.m_ref) | copy-start | bytes 49156
  562.5 14.3 %collective-permute-start.13 = (f32[2,2048]{1,0:T(2,128)}, f32[2,2048]{1,0:T(2,128)S(1)}, u32[]{:S(2)}, u32[]{:S(2)}) collective-permute-start(f32[2,2048]{1,0:T(2,128)} %get-tuple-element.97), channel_id=1, source_target_pairs={{12,0},{16,4},{20,8},{24,12},{28,16},{0,20},{4,24},{8,28},{13,1},{... | collective-permute-start | bytes 49160 | tf_op jit(solution)/shard_map/ppermute | solution.py:641
  565.9 10.9 %collective-permute-start.15 = (f32[2,2048]{1,0:T(2,128)S(1)}, f32[2,2048]{1,0:T(2,128)S(1)}, u32[]{:S(2)}, u32[]{:S(2)}) collective-permute-start(f32[2,2048]{1,0:T(2,128)S(1)} %copy-done.16), channel_id=1, source_target_pairs={{12,0},{16,4},{20,8},{24,12},{28,16},{0,20},{4,24},{8,28},{13,1},{... | collective-permute-start | bytes 49160 | tf_op jit(solution)/shard_map/ppermute | solution.py:641
  576.8 7.5 %copy-start.14 = (f32[2,2048]{1,0:T(2,128)}, f32[2,2048]{1,0:T(2,128)S(1)}, u32[]{:S(2)}) copy-start(f32[2,2048]{1,0:T(2,128)S(1)} %collective-permute-done.13.m_ref) | copy-start | bytes 49156
  576.8 0.7 copy-start.12
  577.5 1.3 copy-start.6
  577.5 6.8 %copy-start.8 = (s16[400,2048]{1,0:T(8,128)(2,1)}, s16[400,2048]{1,0:T(8,128)(2,1)S(1)}, u32[]{:S(2)}) copy-start(s16[400,2048]{1,0:T(8,128)(2,1)S(1)} %collective-permute-done.14.refs_0_) | copy-start | bytes 4915204
  578.7 1.2 copy-start.7
Sparse Core Ops, SparseCore 0:
  455.9 35.1 all-reduce.7
  493.3 56.3 all-gather.1

commit v2 on v1

--- a/solution.py
+++ b/solution.py
@@ -53,6 +53,7 @@
 
 def split_rows(table_t, cols):
     width, rows = table_t.shape
+    rows = round_up(rows, cols)
     return pl.pallas_call(
         functools.partial(split_kernel, width=width, cols=cols),
         grid=(rows // cols,),
@@ -106,7 +107,7 @@
 
 
 def staged(first, u):
-    return pl.ds(PITCH * (first + u), 4)
+    return pl.ds(pl.multiple_of(PITCH * first, 8) + PITCH * u, 4)
 
 
 def column(first, j, size):
@@ -417,36 +418,6 @@
     ]
 
 
-def rotate_kernel(me, x_ref, o_ref):
-    o_ref[...] = x_ref[...]
-
-
-def rotated(x, me, n):
-    block = (x.shape[0] // n, x.shape[1])
-    return pl.pallas_call(
-        rotate_kernel,
-        grid_spec=pltpu.PrefetchScalarGridSpec(
-            num_scalar_prefetch=1,
-            grid=(n,),
-            in_specs=[pl.BlockSpec(block, lambda k, me: (lax.rem(k + me[0], n), 0))],
-            out_specs=pl.BlockSpec(block, lambda k, me: (k, 0)),
-        ),
-        out_shape=jax.ShapeDtypeStruct(x.shape, F32),
-        compiler_params=params(),
-        cost_estimate=cost(0, 8 * x.size),
-        name="rotated",
-    )(me.reshape(1).astype(jnp.int32), x)
-
-
-def summed_blocks(x, axis, held):
-    n = lax.axis_size(axis)
-    rows = x.shape[0] // n
-    total = after(x[:rows], held)
-    for k in range(1, n):
-        total += lax.ppermute(x[k * rows : (k + 1) * rows], axis, [(i, (i + k) % n) for i in range(n)])
-    return total
-
-
 def relation_kernel(g_ref, t_ref, s_ref, _, o_ref, *, width, rows, spare):
     grads = [g_ref[pl.ds(j, rows, stride=4), :] for j in range(4)]
     square = grads[0] * grads[0] + grads[1] * grads[1] + grads[2] * grads[2] + grads[3] * grads[3]
@@ -623,7 +594,7 @@
     return pl.pallas_call(
         functools.partial(decode_kernel, ways=ways),
         grid=(count // cols,),
-        in_specs=[pl.BlockSpec((2, cols), lambda i: (0, i))]
+        in_specs=[pl.BlockSpec((2, cols), lambda i: (0, i + start))]
         + [block] * ways
         + ([] if table_t is None else [pl.BlockSpec(memory_space=pl.ANY)]),
         out_specs=pl.BlockSpec((width, cols), lambda i: (0, i + start)),
@@ -645,26 +616,28 @@
     return [i for i in range(n) if i % 4 == 1]
 
 
-def handed_over(halves, held):
+def handed_over(halves, held, before_meta=()):
     (first, meta_a), (second, meta_b) = halves
     n = lax.axis_size("grp")
     turning = corner_senders(n)
     there = lax.ppermute(first, "grp", [(i, (i + ROUND - 1) % n) for i in turning])
     straight = lax.ppermute(first, "grp", [(i, (i + ROUND) % n) for i in range(n) if i not in turning])
     other = passed_along(second, "grp", ROUND)
-    metas = [passed_along(m, "grp", ROUND) for m in (meta_a, meta_b)]
+    meta = after(jnp.concatenate([meta_a, meta_b], 1), *before_meta)
+    meta = passed_along(meta, "grp", ROUND)
     here = lax.ppermute(
         after(there, *held), "grp", [((i + ROUND - 1) % n, (i + ROUND) % n) for i in turning]
     )
-    return ((straight, here), metas[0]), ((other,), metas[1])
+    return ((straight, here), (other,)), meta, there
 
 
 def decoded(arrived, rows, cols, held):
     table, start = None, 0
-    for codes, meta in arrived:
+    halves, meta = arrived[:2]
+    for codes in halves:
         table = decode((after(codes[0], *held), *codes[1:]), meta, rows, cols, start, table)
         start += codes[0].shape[1] // cols
-    return table, jnp.concatenate([meta[1] for _, meta in arrived])
+    return table, meta[1]
 
 
 def exchanged(blocks):
@@ -708,7 +681,6 @@
     src_idx, rel_idx, tgt_idx = (
         jnp.pad(a, ((0, 0), (0, length - span_len))) for a in (source_rows, relation_ids, target_rows)
     )
-    rel_t_up = jnp.pad(rel_t, ((0, 0), (0, kinds_up - kinds)))
 
     third = -(-spans // 3)
     (c0, c1, c2) = [(a, min(third, spans - a)) for a in range(0, spans, third)]
@@ -719,7 +691,7 @@
     served2 = serve(after(asked_lanes, served1), right_t, *c2)
     left4 = split_rows(after(left_t, served2), 512)
     right4 = split_rows(after(right_t, served2), 512)
-    rel4 = split_rows(after(rel_t_up, served2), kinds_up)
+    rel4 = split_rows(after(rel_t, served2), kinds_up)
 
     fetched1 = exchanged(after(served1, left4, right4, rel4))
     p, pt, src, rel, tgt, gt = edges(
@@ -738,23 +710,23 @@
     gl4, gk4 = sums(gp, src, rel, tgt, totals, sizes, c1[0], c1[1] + c2[1])
 
     returned1 = exchanged(after(gn1, gk4, returned0))
-    rel_rotated = rotated(gk4, lax.axis_index("grp"), lax.axis_size("grp"))
+    rel_total4 = lax.psum_scatter(gk4, "grp", scatter_dimension=0, tiled=True)
     lanes0, lanes1, lanes2 = (
         asked[:, a : a + n].reshape(shards, 1, n * npp) for a, n in (c0, c1, c2)
     )
-    grad_right = spread((), lanes0, after(returned0, rel_rotated), rows, 512)
     blocks = rows // 512
     halves = ((0, blocks // 2), (blocks // 2, blocks - blocks // 2))
-    left_in = after(left_t, grad_right)
+    left_in = after(left_t, gk4)
     coded_left = [tuple(update_left(gl4, left_in, left_state[None], 512, *half)) for half in halves]
-    rel_total4 = summed_blocks(rel_rotated, "grp", coded_left[1][1])
-    rel_sum4 = lax.psum(rel_total4, "shard")
-
-    returned2 = exchanged(after(gn2, rel_total4, returned1))
-    gr4 = target_grads(tgt_idx, live, after(gt, rel_total4, returned1), 4 * rows)
+    left_sent = tuple(c[1] for c in coded_left)
+    gr4 = target_grads(tgt_idx, live, after(gt, *left_sent), 4 * rows)
     moved_left = handed_over(coded_left, (gr4,))
+
+    returned2 = exchanged(after(gn2, gr4, moved_left[2], moved_left[0][0][0], returned1))
+    rel_sum4 = lax.psum(after(rel_total4, gr4), "shard")
+    grad_right = spread((), lanes0, after(returned0, gr4), rows, 512)
     grad_right = spread((grad_right, gr4), lanes1, returned1, rows, 512)
-    grad_right = after(grad_right, *moved_left[0][0], *moved_left[1][0])
+    grad_right = after(grad_right, *moved_left[0][0], *moved_left[0][1], moved_left[1])
 
     coded = []
     for half in halves:
@@ -763,17 +735,17 @@
         )
         grad_right = after(grad_right, coded[-1][1])
     new_left, new_left_state = decoded(moved_left, rows, 512, (coded[1][1],))
-    moved_right = handed_over(coded, (coded[1][1],))
-    new_right, new_right_state = decoded(moved_right, rows, 512, (new_left,))
     slice_rows = kinds_up // lax.axis_size("grp")
     place = lax.axis_index("grp") * slice_rows
     own_rel4 = lax.dynamic_slice(rel4, (4 * place, 0), (4 * slice_rows, LANES))
     own_state = lax.dynamic_slice(
         jnp.pad(relation_state, (0, kinds_up - kinds))[:, None], (place, 0), (slice_rows, 1)
     )
-    new_rel4 = update_relations(rel_sum4, own_rel4, own_state, coded[0][1], width)
+    new_rel4 = update_relations(rel_sum4, own_rel4, own_state, coded[1][1], width)
     new_rel4 = lax.all_gather(new_rel4, "grp", axis=0, tiled=True)
     new_rel_t, new_relation_state = join_relations(new_rel4, width, kinds)
+    moved_right = handed_over(coded, (coded[1][1],), (new_rel_t,))
+    new_right, new_right_state = decoded(moved_right, rows, 512, (new_left, new_rel_t))
     return (new_left.T, new_left_state, new_right.T, new_right_state, new_rel_t.T, new_relation_state[0])
 
 

time: 603 us -> 571 us (0.947)
  starting transfers between devices: 70.4 us -> 49.9 us
  local copies, waits for them, and re-layouts: 22.2 us -> 15.2 us
    ppermute x6 -> x4, waiting for transfers between devices: 26.3 us -> 4.16 us  [passed_along(): return lax.ppermute(block, axis, route)]
    ppermute x2, waiting for transfers between devices: 23.4 us -> 41.5 us  [handed_over(): lax.ppermute(first, 'grp', [(i, (i + ROUND - 1) % n) for i in turning])]
    ppermute x7 -> x0, starting transfers between devices: 13.4 us -> none  [summed_blocks(): lax.ppermute(x[k * rows:(k + 1) * rows], axis, [(i, (i + k) % n) for i in...]
    all_to_all x6, waiting for transfers between devices: 2.88 us -> 15.2 us  [exchanged(): lax.all_to_all(blocks, 'shard', split_axis=0, concat_axis=0, tiled=True)]
    ppermute x6 -> x4, starting transfers between devices: 13.4 us -> 5.46 us  [passed_along(): return lax.ppermute(block, axis, route)]
    psum x1, waiting for transfers between devices: 7.52 us -> 0.01 us  [local(): rel_sum4 = lax.psum(after(rel_total4, gr4), 'shard')]
  transfers between devices with their start and end apart: 27 -> 19, of which waited for: 7 -> 5; matrix products, arithmetic and copies ran while one was open for 3% -> 2% of each run, Pallas kernels for 65% -> 68%
where the time goes in v2:
time: 571 us; the launch traced here: 568 us
  Pallas kernels  412 us (72%)
  waiting for transfers between devices  66.1 us (12%)
  starting transfers between devices  49.9 us (9%)
  local copies, waits for them, and re-layouts  15.2 us (3%)
  between operations  14 us (2%)
  blocking collectives  9.82 us (2%)
    pallas_call x2, Pallas kernels, source_grads(): pl.pallas_call(functools.partial(body, first=first), grid_spec=pltpu.Pref...  87.1 us
    pallas_call x1, Pallas kernels, edges(): pl.pallas_call(edge_kernel, grid_spec=pltpu.PrefetchScalarGridSpec(num_sc...  85.2 us
    pallas_call x3, Pallas kernels, serve(): pl.pallas_call(functools.partial(serve_kernel, rows=rows, step=512), grid...  49.5 us
    pallas_call x3, Pallas kernels, span_grads(): pl.pallas_call(functools.partial(later_span_kernel if later else span_ker...  43.9 us
    ppermute x2, waiting for transfers between devices, handed_over(): lax.ppermute(first, 'grp', [(i, (i + ROUND - 1) % n) for i in turning])  41.5 us
    pallas_call x1, Pallas kernels, target_grads(): pl.pallas_call(target_kernel, grid_spec=pltpu.PrefetchScalarGridSpec(num_...  37.6 us
    pallas_call x2, Pallas kernels, spread(): pl.pallas_call(functools.partial(spread_kernel if grads else first_spread...  30.6 us
    all_to_all x6, starting transfers between devices, exchanged(): lax.all_to_all(blocks, 'shard', split_axis=0, concat_axis=0, tiled=True)  27.7 us
  transfers between devices with their start and end apart: 19, of which 5 were waited for; matrix products, arithmetic and copies ran while one was open for 2% of the time, Pallas kernels for 68%

profile of v2, /device:TPU:1, one launch (start us, length us, event | category | flops | bytes accessed | tf_op | source)
XLA Modules:
  0.0 568.2 jit_solution(9726075786912688858)
XLA Ops:
  8.1 9.8 %all_to_all.35 = s32[4,9,256]{2,1,0:T(8,128)S(1)} all-to-all(s32[4,9,256]{2,1,0:T(8,128)S(1)} %copy.29), channel_id=1, replica_groups=mesh['grp'=8,'shard'=4] {'shard'}, dimensions={0} | all-to-all | bytes 73728 | tf_op jit(solution)/shard_map/all_to_all | solution.py:678
  19.3 16.5 %serve.3 = bf16[4,400,768]{2,1,0:T(8,128)(2,1)} custom-call(s32[4,9,1,256]{3,2,1,0:T(1,128)} %copy.31.idx_ref, f32[400,4096]{1,0:T(8,128)} %bitcast.22), custom_call_target="tpu_custom_call" | custom-call | flops 10066329600 | bytes 6553600 | tf_op jit(solution)/shard_map/serve/pallas_call | solution.py:89
  35.7 3.6 all-to-all-start.1
  40.0 16.5 %serve.4 = bf16[4,400,768]{2,1,0:T(8,128)(2,1)} custom-call(s32[4,9,1,256]{3,2,1,0:T(1,128)} %copy.32.idx_ref, f32[400,4096]{1,0:T(8,128)} %bitcast.23), custom_call_target="tpu_custom_call" | custom-call | flops 10066329600 | bytes 6553600 | tf_op jit(solution)/shard_map/serve/pallas_call | solution.py:89
  57.2 16.5 %serve.5 = bf16[4,400,768]{2,1,0:T(8,128)(2,1)} custom-call(s32[4,9,1,256]{3,2,1,0:T(1,128)} %copy.33.idx_ref, f32[400,4096]{1,0:T(8,128)} %bitcast.24), custom_call_target="tpu_custom_call" | custom-call | flops 10066329600 | bytes 6553600 | tf_op jit(solution)/shard_map/serve/pallas_call | solution.py:89
  73.7 4.0 split_rows.4.rel4
  77.8 9.3 %split_rows.3.left4 = f32[16384,128]{1,0:T(8,128)} custom-call(f32[400,4096]{1,0:T(8,128)} %bitcast.17), custom_call_target="tpu_custom_call" | custom-call | bytes 14942208 | tf_op jit(solution)/shard_map/split_rows/pallas_call | solution.py:57
  87.0 9.4 %split_rows.5.right4 = f32[16384,128]{1,0:T(8,128)} custom-call(f32[400,4096]{1,0:T(8,128)} %bitcast.25), custom_call_target="tpu_custom_call" | custom-call | bytes 14942208 | tf_op jit(solution)/shard_map/split_rows/pallas_call | solution.py:57
  96.4 1.4 copy-done.3
  97.8 4.5 all-to-all-start.3
  104.2 85.2 %edges.1 = (bf16[9,1024,512]{2,1,0:T(8,128)(2,1)}, bf16[9,400,1024]{2,1,0:T(8,128)(2,1)}, f32[9,1024,512]{2,1,0:T(8,128)}, f32[9,1024,512]{2,1,0:T(8,128)}, f32[...) custom-call(s32[9,1024]{1,0:T(8,128)} %pad.18.src_idx, s32[9,1024]{1,0:T(8,128)} %pad.19.rel_idx, s32[9,1024]{1,0:T(8,128)} %pad.21.tgt_idx, ...), custom_call_target="tpu_custom_call" | custom-call | bytes 300000000 | tf_op jit(solution)/shard_map/edges/pallas_call | solution.py:209
  189.4 4.5 all-to-all-start.2
  193.9 14.4 %span_grads.3 = (f32[9,1024,512]{2,1,0:T(8,128)}, bf16[4,400,768]{2,1,0:T(8,128)(2,1)}) custom-call(s32[9]{0:T(128)} %bitcast.35, bf16[4,400,768]{2,1,0:T(8,128)(2,1)} %copy-done.3, bf16[9,1024,512]{2,1,0:T(8,128)(2,1)} %get-tuple-element.64.p_ref, bf16[9,400,1024]{2,1,0:T(8,128)(2,1)} %get-tuple-element.66.pt_ref), custom_call_target="tpu_custom_call" | custom-call | flops 9663676416 | bytes 12582912 | tf_op jit(solution)/shard_map/span_grads/pallas_call | solution.py:306
  208.3 13.4 %span_grads.4 = (f32[9,1024,512]{2,1,0:T(8,128)}, bf16[4,400,768]{2,1,0:T(8,128)(2,1)}) custom-call(s32[9]{0:T(128)} %bitcast.36, bf16[4,400,768]{2,1,0:T(8,128)(2,1)} %copy-done, bf16[9,1024,512]{2,1,0:T(8,128)(2,1)} %get-tuple-element.64.p_ref, bf16[9,400,1024]{2,1,0:T(8,128)(2,1)} %get-tuple-element.66.pt_ref, ...), custom_call_target="tpu_custom_call", output_to_operand_aliasing={{0}: (4, {})} | custom-call | flops 9663676416 | bytes 12582912 | tf_op jit(solution)/shard_map/span_grads/pallas_call | solution.py:306
  221.7 30.5 %source_grads.2 = (f32[16384,128]{1,0:T(8,128)}, f32[5632,128]{1,0:T(8,128)}) custom-call(s32[9,1024]{1,0:T(8,128)} %pad.18.src_idx, s32[9,1024]{1,0:T(8,128)} %pad.19.rel_idx, s32[9]{0:T(128)} %bitcast.37, f32[9,1024,512]{2,1,0:T(8,128)} %get-tuple-element.75.gp._, f32[9,1024,512]{2,1,0:T(8,128)} %get-tuple-element.71.src.src_ref, ...), custom_call_target="tpu_custom_call" | custom-call | bytes 90000000 | tf_op jit(solution)/shard_map/source_grads/pallas_call | solution.py:398
  252.2 6.8 %all-to-all-start.4 = ((bf16[4,400,768]{2,1,0:T(8,128)(2,1)}), bf16[4,400,768]{2,1,0:T(8,128)(2,1)S(1)}, u32[]{:S(2)}, u32[]{:S(2)}) async-start(bf16[4,400,768]{2,1,0:T(8,128)(2,1)} %get-tuple-element.85), calls=%async_computation.4 | async-start | bytes 4915200 | tf_op jit(solution)/shard_map/all_to_all | solution.py:644
  259.0 16.2 %span_grads.5 = (f32[9,1024,512]{2,1,0:T(8,128)}, bf16[4,400,768]{2,1,0:T(8,128)(2,1)}) custom-call(s32[9]{0:T(128)} %bitcast.38, bf16[4,400,768]{2,1,0:T(8,128)(2,1)} %all-to-all-done.2.neg_ref, bf16[9,1024,512]{2,1,0:T(8,128)(2,1)} %get-tuple-element.64.p_ref, bf16[9,400,1024]{2,1,0:T(8,128)(2,1)} %get-tuple-element.66.pt_ref, ...), custom_call_target="tpu_custom_call", output_to_operand_aliasing={{0}: (4, {})} | custom-call | flops 9663676416 | bytes 12582912 | tf_op jit(solution)/shard_map/span_grads/pallas_call | solution.py:306
  275.1 56.6 %source_grads.3 = (f32[16384,128]{1,0:T(8,128)}, f32[5632,128]{1,0:T(8,128)}) custom-call(s32[9,1024]{1,0:T(8,128)} %pad.18.src_idx, s32[9,1024]{1,0:T(8,128)} %pad.19.rel_idx, s32[9]{0:T(128)} %bitcast.39, f32[9,1024,512]{2,1,0:T(8,128)} %get-tuple-element.76.gp_ref, f32[9,1024,512]{2,1,0:T(8,128)} %get-tuple-element.71.src.src_ref, ...), custom_call_target="tpu_custom_call" | custom-call | bytes 180000000 | tf_op jit(solution)/shard_map/source_grads/pallas_call | solution.py:398
  331.7 4.5 all-to-all-start.5
  336.3 5.8 %update_left.2 = (s16[400,2048]{1,0:T(8,128)(2,1)}, f32[2,2048]{1,0:T(2,128)}) custom-call(f32[16384,128]{1,0:T(8,128)} %get-tuple-element.78.g_ref, f32[400,4096]{1,0:T(8,128)} %bitcast.18, f32[1,4096]{1,0:T(1,128)} %bitcast.32), custom_call_target="tpu_custom_call" | custom-call | bytes 8192000 | tf_op jit(solution)/shard_map/update_left/pallas_call | solution.py:497
  342.2 5.7 %collective-permute-start.3 = (s16[400,2048]{1,0:T(8,128)(2,1)}, s16[400,2048]{1,0:T(8,128)(2,1)}, u32[]{:S(2)}, u32[]{:S(2)}) collective-permute-start(s16[400,2048]{1,0:T(8,128)(2,1)} %get-tuple-element.91), channel_id=1, source_target_pairs={{4,20},{20,4},{5,21},{21,5},{6,22},{22,6},{7,23},{23,7}} | collective-permute-start | bytes 4915208 | tf_op jit(solution)/shard_map/ppermute | solution.py:623
  347.9 1.5 collective-permute-start.2
  349.4 5.8 %update_left.3 = (s16[400,2048]{1,0:T(8,128)(2,1)}, f32[2,2048]{1,0:T(2,128)}) custom-call(f32[16384,128]{1,0:T(8,128)} %get-tuple-element.78.g_ref, f32[400,4096]{1,0:T(8,128)} %bitcast.19, f32[1,4096]{1,0:T(1,128)} %bitcast.33), custom_call_target="tpu_custom_call" | custom-call | bytes 8192000 | tf_op jit(solution)/shard_map/update_left/pallas_call | solution.py:497
  355.1 37.6 %target_grads.1.g4_ref = f32[16384,128]{1,0:T(8,128)} custom-call(s32[9,1024]{1,0:T(8,128)} %pad.21.tgt_idx, s32[9]{0:T(128)} %bitcast.40, f32[46080,128]{1,0:T(8,128)} %get-tuple-element.87.gt_ref), custom_call_target="tpu_custom_call" | custom-call | bytes 100000000 | tf_op jit(solution)/shard_map/target_grads/pallas_call | solution.py:257
  392.8 1.1 copy-done.4
  394.0 3.7 all-to-all-start.6
  400.4 1.7 constant_dynamic-slice_fusion.t_ref
  402.2 5.3 collective-permute-start
  407.6 2.5 collective-permute-start.4
  410.1 14.4 %spread.2.g_ref = f32[400,4096]{1,0:T(8,128)} custom-call(s32[4,1,768]{2,1,0:T(1,128)} %reshape.33.idx_ref, bf16[4,400,768]{2,1,0:T(8,128)(2,1)} %copy-done.1), custom_call_target="tpu_custom_call" | custom-call | flops 10066329600 | bytes 13107200 | tf_op jit(solution)/shard_map/spread/pallas_call | solution.py:548
  424.6 16.2 %spread.3.g_ref = f32[400,4096]{1,0:T(8,128)} custom-call(f32[400,4096]{1,0:T(8,128)} %spread.2.g_ref, f32[16384,128]{1,0:T(8,128)} %target_grads.1.g4_ref, s32[4,1,768]{2,1,0:T(1,128)} %reshape.34.idx_ref, bf16[4,400,768]{2,1,0:T(8,128)(2,1)} %all-to-all-done.5.b_ref), custom_call_target="tpu_custom_call" | custom-call | flops 10066329600 | bytes 13107200 | tf_op jit(solution)/shard_map/spread/pallas_call | solution.py:548
  440.8 2.9 collective-permute-done.4.refs_1_
  443.7 15.1 %all-to-all-done.6.b_ref = bf16[4,400,768]{2,1,0:T(8,128)(2,1)S(1)} async-done(((bf16[4,400,768]{2,1,0:T(8,128)(2,1)}), bf16[4,400,768]{2,1,0:T(8,128)(2,1)S(1)}, u32[]{:S(2)}, u32[]{:S(2)}) %all-to-all-start.6) | async-done | bytes 2457632 | tf_op jit(solution)/shard_map/all_to_all | solution.py:644
  458.8 1.4 copy-done.2
  460.3 10.4 %spread_update.2 = (s16[400,2048]{1,0:T(8,128)(2,1)}, f32[2,2048]{1,0:T(2,128)}) custom-call(f32[400,4096]{1,0:T(8,128)} %spread.3.g_ref, s32[4,1,768]{2,1,0:T(1,128)} %reshape.35.idx_ref, bf16[4,400,768]{2,1,0:T(8,128)(2,1)} %copy-done.2, f32[400,4096]{1,0:T(8,128)} %bitcast.26, f32[1,4096]{1,0:T(1,128)} %bitcast.45), custom_call_target="tpu_custom_call" | custom-call | flops 5033164800 | bytes 6553600 | tf_op jit(solution)/shard_map/spread_update/pallas_call | solution.py:568
  470.6 10.4 %spread_update.3 = (s16[400,2048]{1,0:T(8,128)(2,1)}, f32[2,2048]{1,0:T(2,128)}) custom-call(f32[400,4096]{1,0:T(8,128)} %spread.3.g_ref, s32[4,1,768]{2,1,0:T(1,128)} %reshape.35.idx_ref, bf16[4,400,768]{2,1,0:T(8,128)(2,1)} %copy-done.2, f32[400,4096]{1,0:T(8,128)} %bitcast.27, f32[1,4096]{1,0:T(1,128)} %bitcast.46), custom_call_target="tpu_custom_call" | custom-call | flops 5033164800 | bytes 6553600 | tf_op jit(solution)/shard_map/spread_update/pallas_call | solution.py:568
  481.1 2.1 update_relations.1
  483.2 3.2 collective-permute-start.8
  486.4 1.3 collective-permute-start.7
  487.8 41.5 %collective-permute-done.8 = s16[400,2048]{1,0:T(8,128)(2,1)} collective-permute-done((s16[400,2048]{1,0:T(8,128)(2,1)}, s16[400,2048]{1,0:T(8,128)(2,1)}, u32[]{:S(2)}, u32[]{:S(2)}) %collective-permute-start.8) | collective-permute-done | bytes 1638432 | tf_op jit(solution)/shard_map/ppermute | solution.py:623
  529.3 2.5 collective-permute-start.9
  532.5 2.3 all-gather.2.cloned.1.call-done.g_ref
  534.8 4.0 join_relations.1
  539.4 4.4 decode.4.refs_1_
  543.8 4.0 decode.5
  547.8 4.1 collective-permute-done.6.refs_0_
  553.3 4.4 decode.6.refs_1_
  557.7 4.0 decode.7
  (79 shorter events, 11.2 us)
Async XLA Ops:
  18.0 0.6 copy-start.7
  35.7 60.7 %all-to-all-start.1 = ((bf16[4,400,768]{2,1,0:T(8,128)(2,1)}), bf16[4,400,768]{2,1,0:T(8,128)(2,1)S(1)}, u32[]{:S(2)}, u32[]{:S(2)}) async-start(bf16[4,400,768]{2,1,0:T(8,128)(2,1)} %serve.3), calls=%async_computation.1 | async-start | bytes 4915200 | tf_op jit(solution)/shard_map/all_to_all | solution.py:644
  96.4 5.9 %copy-start.11 = (s32[9,1000]{1,0:T(8,128)S(1)}, s32[9,1000]{1,0:T(8,128)}, u32[]{:S(2)}) copy-start(s32[9,1000]{1,0:T(8,128)} %param.17) | copy-start | bytes 108004
  96.4 6.6 %copy-start.12 = (s32[9,1000]{1,0:T(8,128)S(1)}, s32[9,1000]{1,0:T(8,128)}, u32[]{:S(2)}) copy-start(s32[9,1000]{1,0:T(8,128)} %param.18) | copy-start | bytes 108004
  96.4 7.2 %copy-start.13 = (s32[9,1000]{1,0:T(8,128)S(1)}, s32[9,1000]{1,0:T(8,128)}, u32[]{:S(2)}) copy-start(s32[9,1000]{1,0:T(8,128)} %param.19) | copy-start | bytes 108004
  96.4 1.4 copy-start.3
  97.8 91.6 %all-to-all-start.3 = ((bf16[4,400,768]{2,1,0:T(8,128)(2,1)}), bf16[4,400,768]{2,1,0:T(8,128)(2,1)S(1)}, u32[]{:S(2)}, u32[]{:S(2)}) async-start(bf16[4,400,768]{2,1,0:T(8,128)(2,1)} %serve.4), calls=%async_computation.3 | async-start | bytes 4915200 | tf_op jit(solution)/shard_map/all_to_all | solution.py:644
  189.4 18.9 %copy-start = (bf16[4,400,768]{2,1,0:T(8,128)(2,1)}, bf16[4,400,768]{2,1,0:T(8,128)(2,1)S(1)}, u32[]{:S(2)}) copy-start(bf16[4,400,768]{2,1,0:T(8,128)(2,1)S(1)} %all-to-all-done.3.neg_ref) | copy-start | bytes 7372804
  189.4 62.8 %all-to-all-start.2 = ((bf16[4,400,768]{2,1,0:T(8,128)(2,1)}), bf16[4,400,768]{2,1,0:T(8,128)(2,1)}, u32[]{:S(2)}, u32[]{:S(2)}) async-start(bf16[4,400,768]{2,1,0:T(8,128)(2,1)} %serve.5), calls=%async_computation.2 | async-start | bytes 4915200 | tf_op jit(solution)/shard_map/all_to_all | solution.py:644
  252.2 79.5 %all-to-all-start.4 = ((bf16[4,400,768]{2,1,0:T(8,128)(2,1)}), bf16[4,400,768]{2,1,0:T(8,128)(2,1)S(1)}, u32[]{:S(2)}, u32[]{:S(2)}) async-start(bf16[4,400,768]{2,1,0:T(8,128)(2,1)} %get-tuple-element.85), calls=%async_computation.4 | async-start | bytes 4915200 | tf_op jit(solution)/shard_map/all_to_all | solution.py:644
  331.7 10.4 %copy-start.1 = (bf16[4,400,768]{2,1,0:T(8,128)(2,1)}, bf16[4,400,768]{2,1,0:T(8,128)(2,1)S(1)}, u32[]{:S(2)}) copy-start(bf16[4,400,768]{2,1,0:T(8,128)(2,1)S(1)} %all-to-all-done.4.b_ref) | copy-start | bytes 7372804
  331.7 61.1 %all-to-all-start.5 = ((bf16[4,400,768]{2,1,0:T(8,128)(2,1)}), bf16[4,400,768]{2,1,0:T(8,128)(2,1)}, u32[]{:S(2)}, u32[]{:S(2)}) async-start(bf16[4,400,768]{2,1,0:T(8,128)(2,1)} %get-tuple-element.90), calls=%async_computation.5 | async-start | bytes 4915200 | tf_op jit(solution)/shard_map/all_to_all | solution.py:644
  336.3 88.3 %reduce-scatter.2.cloned.1.call-start = ((), (), s32[]{:S(2)}) async-start(), calls=%async_computation.8 | async-start | bytes 3244032 | tf_op jit(solution)/shard_map/reduce_scatter | solution.py:713
  342.2 50.6 %collective-permute-start.3 = (s16[400,2048]{1,0:T(8,128)(2,1)}, s16[400,2048]{1,0:T(8,128)(2,1)}, u32[]{:S(2)}, u32[]{:S(2)}) collective-permute-start(s16[400,2048]{1,0:T(8,128)(2,1)} %get-tuple-element.91), channel_id=1, source_target_pairs={{4,20},{20,4},{5,21},{21,5},{6,22},{22,6},{7,23},{23,7}} | collective-permute-start | bytes 4915208 | tf_op jit(solution)/shard_map/ppermute | solution.py:623
  347.9 44.9 %collective-permute-start.2 = (s16[400,2048]{1,0:T(8,128)(2,1)}, s16[400,2048]{1,0:T(8,128)(2,1)S(1)}, u32[]{:S(2)}, u32[]{:S(2)}) collective-permute-start(s16[400,2048]{1,0:T(8,128)(2,1)} %get-tuple-element.91), channel_id=1, source_target_pairs={{0,20},{8,28},{12,0},{16,4},{24,12},{28,16},{1,21},{9,29},{13,1},{... | collective-permute-start | bytes 4915208 | tf_op jit(solution)/shard_map/ppermute | solution.py:624
  392.8 4.9 copy-start.17
  392.8 5.8 %copy-start.8 = (s32[4,9,256]{2,1,0:T(8,128)S(1)}, s32[4,9,256]{2,1,0:T(8,128)}, u32[]{:S(2)}) copy-start(s32[4,9,256]{2,1,0:T(8,128)} %copy-done.7) | copy-start | bytes 110596
  392.8 1.2 copy-start.4
  392.8 9.4 %copy-start.14 = (f32[2,2048]{1,0:T(2,128)S(1)}, f32[2,2048]{1,0:T(2,128)}, u32[]{:S(2)}) copy-start(f32[2,2048]{1,0:T(2,128)} %get-tuple-element.81) | copy-start | bytes 49156
  392.8 9.4 %copy-start.15 = (f32[2,2048]{1,0:T(2,128)S(1)}, f32[2,2048]{1,0:T(2,128)}, u32[]{:S(2)}) copy-start(f32[2,2048]{1,0:T(2,128)} %get-tuple-element.82) | copy-start | bytes 49156
  394.0 64.9 %all-to-all-start.6 = ((bf16[4,400,768]{2,1,0:T(8,128)(2,1)}), bf16[4,400,768]{2,1,0:T(8,128)(2,1)S(1)}, u32[]{:S(2)}, u32[]{:S(2)}) async-start(bf16[4,400,768]{2,1,0:T(8,128)(2,1)} %get-tuple-element.95), calls=%async_computation.6 | async-start | bytes 4915200 | tf_op jit(solution)/shard_map/all_to_all | solution.py:644
  397.7 83.4 %all-reduce.7.cloned.1.call-start = ((), (), s32[]{:S(2)}) async-start(), calls=%async_computation.9 | async-start | bytes 720896 | tf_op jit(solution)/shard_map/psum | solution.py:726
  402.2 38.6 %collective-permute-start = (f32[2,4096]{1,0:T(2,128)S(1)}, f32[2,4096]{1,0:T(2,128)S(1)}, u32[]{:S(2)}, u32[]{:S(2)}) collective-permute-start(f32[2,4096]{1,0:T(2,128)S(1)} %pad_maximum_fusion), channel_id=1, source_target_pairs={{12,0},{16,4},{20,8},{24,12},{28,16},{0,20},{4,24},{8,28},{13,1},{... | collective-permute-start | bytes 98312 | tf_op jit(solution)/shard_map/ppermute | solution.py:612
  407.5 33.2 %collective-permute-start.1 = (s16[400,2048]{1,0:T(8,128)(2,1)}, s16[400,2048]{1,0:T(8,128)(2,1)}, u32[]{:S(2)}, u32[]{:S(2)}) collective-permute-start(s16[400,2048]{1,0:T(8,128)(2,1)} %get-tuple-element.83), channel_id=1, source_target_pairs={{12,0},{16,4},{20,8},{24,12},{28,16},{0,20},{4,24},{8,28},{13,1},{... | collective-permute-start | bytes 4915208 | tf_op jit(solution)/shard_map/ppermute | solution.py:612
  407.6 36.1 %collective-permute-start.4 = (s16[400,2048]{1,0:T(8,128)(2,1)}, s16[400,2048]{1,0:T(8,128)(2,1)}, u32[]{:S(2)}, u32[]{:S(2)}) collective-permute-start(s16[400,2048]{1,0:T(8,128)(2,1)} %collective-permute-done.3), channel_id=1, source_target_pairs={{20,24},{4,8},{21,25},{5,9},{22,26},{6,10},{23,27},{7,11}} | collective-permute-start | bytes 4915208 | tf_op jit(solution)/shard_map/ppermute | solution.py:628
  424.6 110.2 %all-gather.2.cloned.1.call-start = ((), (), s32[]{:S(2)}) async-start(), calls=%async_computation.10 | async-start | bytes 3244032 | tf_op jit(solution)/shard_map/all_gather | solution.py:745
  440.8 98.0 %copy-start.9 = (f32[2,4096]{1,0:T(2,128)}, f32[2,4096]{1,0:T(2,128)S(1)}, u32[]{:S(2)}) copy-start(f32[2,4096]{1,0:T(2,128)S(1)} %collective-permute-done.m_ref) | copy-start | bytes 98308
  458.8 1.4 copy-start.2
  470.6 61.1 %copy-start.16 = (f32[2,2048]{1,0:T(2,128)S(1)}, f32[2,2048]{1,0:T(2,128)}, u32[]{:S(2)}) copy-start(f32[2,2048]{1,0:T(2,128)} %get-tuple-element.96) | copy-start | bytes 49156
  483.2 46.1 %collective-permute-start.8 = (s16[400,2048]{1,0:T(8,128)(2,1)}, s16[400,2048]{1,0:T(8,128)(2,1)}, u32[]{:S(2)}, u32[]{:S(2)}) collective-permute-start(s16[400,2048]{1,0:T(8,128)(2,1)} %get-tuple-element.106), channel_id=1, source_target_pairs={{4,20},{20,4},{5,21},{21,5},{6,22},{22,6},{7,23},{23,7}} | collective-permute-start | bytes 4915208 | tf_op jit(solution)/shard_map/ppermute | solution.py:623
  486.4 61.4 %collective-permute-start.7 = (s16[400,2048]{1,0:T(8,128)(2,1)}, s16[400,2048]{1,0:T(8,128)(2,1)S(1)}, u32[]{:S(2)}, u32[]{:S(2)}) collective-permute-start(s16[400,2048]{1,0:T(8,128)(2,1)} %get-tuple-element.106), channel_id=1, source_target_pairs={{0,20},{8,28},{12,0},{16,4},{24,12},{28,16},{1,21},{9,29},{13,1},{... | collective-permute-start | bytes 4915208 | tf_op jit(solution)/shard_map/ppermute | solution.py:624
  487.7 64.2 %collective-permute-start.6 = (s16[400,2048]{1,0:T(8,128)(2,1)}, s16[400,2048]{1,0:T(8,128)(2,1)S(1)}, u32[]{:S(2)}, u32[]{:S(2)}) collective-permute-start(s16[400,2048]{1,0:T(8,128)(2,1)} %get-tuple-element.104), channel_id=1, source_target_pairs={{12,0},{16,4},{20,8},{24,12},{28,16},{0,20},{4,24},{8,28},{13,1},{... | collective-permute-start | bytes 4915208 | tf_op jit(solution)/shard_map/ppermute | solution.py:612
  529.3 24.0 %collective-permute-start.9 = (s16[400,2048]{1,0:T(8,128)(2,1)}, s16[400,2048]{1,0:T(8,128)(2,1)}, u32[]{:S(2)}, u32[]{:S(2)}) collective-permute-start(s16[400,2048]{1,0:T(8,128)(2,1)} %collective-permute-done.8), channel_id=1, source_target_pairs={{20,24},{4,8},{21,25},{5,9},{22,26},{6,10},{23,27},{7,11}} | collective-permute-start | bytes 4915208 | tf_op jit(solution)/shard_map/ppermute | solution.py:628
  538.8 13.8 %collective-permute-start.5 = (f32[2,4096]{1,0:T(2,128)S(1)}, f32[2,4096]{1,0:T(2,128)S(1)}, u32[]{:S(2)}, u32[]{:S(2)}) collective-permute-start(f32[2,4096]{1,0:T(2,128)S(1)} %pad_maximum_fusion.1), channel_id=1, source_target_pairs={{12,0},{16,4},{20,8},{24,12},{28,16},{0,20},{4,24},{8,28},{13,1},{... | collective-permute-start | bytes 98312 | tf_op jit(solution)/shard_map/ppermute | solution.py:612
  543.8 8.2 %copy-start.18 = (f32[1,1345]{1,0:T(1,128)S(1)}, f32[1,1345]{1,0:T(1,128)}, u32[]{:S(2)}) copy-start(f32[1,1345]{1,0:T(1,128)} %get-tuple-element.109) | copy-start | bytes 16144
  547.8 5.5 copy-start.5
  552.0 5.7 %copy-start.6 = (s16[400,2048]{1,0:T(8,128)(2,1)}, s16[400,2048]{1,0:T(8,128)(2,1)S(1)}, u32[]{:S(2)}) copy-start(s16[400,2048]{1,0:T(8,128)(2,1)S(1)} %collective-permute-done.6.refs_0_) | copy-start | bytes 4915204
  552.6 0.6 copy-start.10
Sparse Core Ops, SparseCore 0:
  349.5 53.4 reduce-scatter.1
  424.7 51.4 all-reduce.6
  483.3 51.4 all-gather.1

commit v3 on v2

--- a/solution.py
+++ b/solution.py
@@ -12,7 +12,7 @@
 EPSILON = 1e-08
 LANES = 128
 TILE = 256
-GROUP = 16
+GROUP = 32
 PITCH = 5
 CODE = 32767.0
 VMEM_LIMIT = 58 * 1024 * 1024

time: 571 us -> 572 us (level)
  Pallas kernels: 412 us -> 393 us
  starting transfers between devices: 49.9 us -> 64.6 us
    pallas_call x2, Pallas kernels: 87.1 us -> 79.3 us  [source_grads(): pl.pallas_call(functools.partial(body, first=first), grid_spec=pltpu.Pref...]
    ppermute x2, starting transfers between devices: 8.92 us -> 16.4 us  [handed_over(): lax.ppermute(first, 'grp', [(i, (i + ROUND - 1) % n) for i in turning])]
    all_to_all x6, starting transfers between devices: 27.7 us -> 35.1 us  [exchanged(): lax.all_to_all(blocks, 'shard', split_axis=0, concat_axis=0, tiled=True)]
    pallas_call x1, Pallas kernels: 85.2 us -> 78.5 us  [edges(): pl.pallas_call(edge_kernel, grid_spec=pltpu.PrefetchScalarGridSpec(num_sc...]
  transfers between devices with their start and end apart: 19 -> 19, of which waited for: 5 -> 7; matrix products, arithmetic and copies ran while one was open for 2% -> 2% of each run, Pallas kernels for 68% -> 64%
where the time goes in v3:
time: 572 us; the launch traced here: 568 us
  Pallas kernels  393 us (69%)
  waiting for transfers between devices  70.3 us (12%)
  starting transfers between devices  64.6 us (11%)
  local copies, waits for them, and re-layouts  15.2 us (3%)
  between operations  13.9 us (2%)
  blocking collectives  9.82 us (2%)
    pallas_call x2, Pallas kernels, source_grads(): pl.pallas_call(functools.partial(body, first=first), grid_spec=pltpu.Pref...  79.3 us
    pallas_call x1, Pallas kernels, edges(): pl.pallas_call(edge_kernel, grid_spec=pltpu.PrefetchScalarGridSpec(num_sc...  78.5 us
    pallas_call x3, Pallas kernels, serve(): pl.pallas_call(functools.partial(serve_kernel, rows=rows, step=512), grid...  49.5 us
    pallas_call x3, Pallas kernels, span_grads(): pl.pallas_call(functools.partial(later_span_kernel if later else span_ker...  43.5 us
    ppermute x2, waiting for transfers between devices, handed_over(): lax.ppermute(first, 'grp', [(i, (i + ROUND - 1) % n) for i in turning])  42.1 us
    all_to_all x6, starting transfers between devices, exchanged(): lax.all_to_all(blocks, 'shard', split_axis=0, concat_axis=0, tiled=True)  35.1 us
    pallas_call x1, Pallas kernels, target_grads(): pl.pallas_call(target_kernel, grid_spec=pltpu.PrefetchScalarGridSpec(num_...  33.6 us
    pallas_call x2, Pallas kernels, spread(): pl.pallas_call(functools.partial(spread_kernel if grads else first_spread...  30.6 us
  transfers between devices with their start and end apart: 19, of which 7 were waited for; matrix products, arithmetic and copies ran while one was open for 2% of the time, Pallas kernels for 64%

profile of v3, /device:TPU:1, one launch (start us, length us, event | category | flops | bytes accessed | tf_op | source)
XLA Modules:
  0.0 568.2 jit_solution(1193714933836378919)
XLA Ops:
  7.2 0.9 reshape.28
  8.1 9.8 %all_to_all.35 = s32[4,9,256]{2,1,0:T(8,128)S(1)} all-to-all(s32[4,9,256]{2,1,0:T(8,128)S(1)} %copy.29), channel_id=1, replica_groups=mesh['grp'=8,'shard'=4] {'shard'}, dimensions={0} | all-to-all | bytes 73728 | tf_op jit(solution)/shard_map/all_to_all | solution.py:678
  19.3 16.5 %serve.3 = bf16[4,400,768]{2,1,0:T(8,128)(2,1)} custom-call(s32[4,9,1,256]{3,2,1,0:T(1,128)} %copy.31.idx_ref, f32[400,4096]{1,0:T(8,128)} %bitcast.22), custom_call_target="tpu_custom_call" | custom-call | flops 10066329600 | bytes 6553600 | tf_op jit(solution)/shard_map/serve/pallas_call | solution.py:89
  35.7 3.6 all-to-all-start.1
  40.0 16.5 %serve.4 = bf16[4,400,768]{2,1,0:T(8,128)(2,1)} custom-call(s32[4,9,1,256]{3,2,1,0:T(1,128)} %copy.32.idx_ref, f32[400,4096]{1,0:T(8,128)} %bitcast.23), custom_call_target="tpu_custom_call" | custom-call | flops 10066329600 | bytes 6553600 | tf_op jit(solution)/shard_map/serve/pallas_call | solution.py:89
  57.2 16.5 %serve.5 = bf16[4,400,768]{2,1,0:T(8,128)(2,1)} custom-call(s32[4,9,1,256]{3,2,1,0:T(1,128)} %copy.33.idx_ref, f32[400,4096]{1,0:T(8,128)} %bitcast.24), custom_call_target="tpu_custom_call" | custom-call | flops 10066329600 | bytes 6553600 | tf_op jit(solution)/shard_map/serve/pallas_call | solution.py:89
  73.7 4.0 split_rows.4.rel4
  77.8 9.3 %split_rows.3.left4 = f32[16384,128]{1,0:T(8,128)} custom-call(f32[400,4096]{1,0:T(8,128)} %bitcast.17), custom_call_target="tpu_custom_call" | custom-call | bytes 14942208 | tf_op jit(solution)/shard_map/split_rows/pallas_call | solution.py:57
  87.0 9.4 %split_rows.5.right4 = f32[16384,128]{1,0:T(8,128)} custom-call(f32[400,4096]{1,0:T(8,128)} %bitcast.25), custom_call_target="tpu_custom_call" | custom-call | bytes 14942208 | tf_op jit(solution)/shard_map/split_rows/pallas_call | solution.py:57
  96.4 1.4 copy-done.3
  97.8 4.5 all-to-all-start.3
  104.2 78.5 %edges.1 = (bf16[9,1024,512]{2,1,0:T(8,128)(2,1)}, bf16[9,400,1024]{2,1,0:T(8,128)(2,1)}, f32[9,1024,512]{2,1,0:T(8,128)}, f32[9,1024,512]{2,1,0:T(8,128)}, f32[...) custom-call(s32[9,1024]{1,0:T(8,128)} %pad.18.src_idx, s32[9,1024]{1,0:T(8,128)} %pad.19.rel_idx, s32[9,1024]{1,0:T(8,128)} %pad.21.tgt_idx, ...), custom_call_target="tpu_custom_call" | custom-call | bytes 300000000 | tf_op jit(solution)/shard_map/edges/pallas_call | solution.py:209
  182.8 9.4 %all-to-all-start.2 = ((bf16[4,400,768]{2,1,0:T(8,128)(2,1)}), bf16[4,400,768]{2,1,0:T(8,128)(2,1)}, u32[]{:S(2)}, u32[]{:S(2)}) async-start(bf16[4,400,768]{2,1,0:T(8,128)(2,1)} %serve.5), calls=%async_computation.2 | async-start | bytes 4915200 | tf_op jit(solution)/shard_map/all_to_all | solution.py:644
  192.2 12.5 %span_grads.3 = (f32[9,1024,512]{2,1,0:T(8,128)}, bf16[4,400,768]{2,1,0:T(8,128)(2,1)}) custom-call(s32[9]{0:T(128)} %bitcast.35, bf16[4,400,768]{2,1,0:T(8,128)(2,1)} %copy-done.3, bf16[9,1024,512]{2,1,0:T(8,128)(2,1)} %get-tuple-element.64.p_ref, bf16[9,400,1024]{2,1,0:T(8,128)(2,1)} %get-tuple-element.66.pt_ref), custom_call_target="tpu_custom_call" | custom-call | flops 9663676416 | bytes 12582912 | tf_op jit(solution)/shard_map/span_grads/pallas_call | solution.py:306
  204.7 16.2 %span_grads.4 = (f32[9,1024,512]{2,1,0:T(8,128)}, bf16[4,400,768]{2,1,0:T(8,128)(2,1)}) custom-call(s32[9]{0:T(128)} %bitcast.36, bf16[4,400,768]{2,1,0:T(8,128)(2,1)} %copy-done, bf16[9,1024,512]{2,1,0:T(8,128)(2,1)} %get-tuple-element.64.p_ref, bf16[9,400,1024]{2,1,0:T(8,128)(2,1)} %get-tuple-element.66.pt_ref, ...), custom_call_target="tpu_custom_call", output_to_operand_aliasing={{0}: (4, {})} | custom-call | flops 9663676416 | bytes 12582912 | tf_op jit(solution)/shard_map/span_grads/pallas_call | solution.py:306
  220.9 26.0 %source_grads.2 = (f32[16384,128]{1,0:T(8,128)}, f32[5632,128]{1,0:T(8,128)}) custom-call(s32[9,1024]{1,0:T(8,128)} %pad.18.src_idx, s32[9,1024]{1,0:T(8,128)} %pad.19.rel_idx, s32[9]{0:T(128)} %bitcast.37, f32[9,1024,512]{2,1,0:T(8,128)} %get-tuple-element.75.gp._, f32[9,1024,512]{2,1,0:T(8,128)} %get-tuple-element.71.src.src_ref, ...), custom_call_target="tpu_custom_call" | custom-call | bytes 90000000 | tf_op jit(solution)/shard_map/source_grads/pallas_call | solution.py:398
  247.7 8.4 %all-to-all-start.4 = ((bf16[4,400,768]{2,1,0:T(8,128)(2,1)}), bf16[4,400,768]{2,1,0:T(8,128)(2,1)S(1)}, u32[]{:S(2)}, u32[]{:S(2)}) async-start(bf16[4,400,768]{2,1,0:T(8,128)(2,1)} %get-tuple-element.85), calls=%async_computation.4 | async-start | bytes 4915200 | tf_op jit(solution)/shard_map/all_to_all | solution.py:644
  256.0 14.8 %span_grads.5 = (f32[9,1024,512]{2,1,0:T(8,128)}, bf16[4,400,768]{2,1,0:T(8,128)(2,1)}) custom-call(s32[9]{0:T(128)} %bitcast.38, bf16[4,400,768]{2,1,0:T(8,128)(2,1)} %all-to-all-done.2.neg_ref, bf16[9,1024,512]{2,1,0:T(8,128)(2,1)} %get-tuple-element.64.p_ref, bf16[9,400,1024]{2,1,0:T(8,128)(2,1)} %get-tuple-element.66.pt_ref, ...), custom_call_target="tpu_custom_call", output_to_operand_aliasing={{0}: (4, {})} | custom-call | flops 9663676416 | bytes 12582912 | tf_op jit(solution)/shard_map/span_grads/pallas_call | solution.py:306
  270.9 53.3 %source_grads.3 = (f32[16384,128]{1,0:T(8,128)}, f32[5632,128]{1,0:T(8,128)}) custom-call(s32[9,1024]{1,0:T(8,128)} %pad.18.src_idx, s32[9,1024]{1,0:T(8,128)} %pad.19.rel_idx, s32[9]{0:T(128)} %bitcast.39, f32[9,1024,512]{2,1,0:T(8,128)} %get-tuple-element.76.gp_ref, f32[9,1024,512]{2,1,0:T(8,128)} %get-tuple-element.71.src.src_ref, ...), custom_call_target="tpu_custom_call" | custom-call | bytes 180000000 | tf_op jit(solution)/shard_map/source_grads/pallas_call | solution.py:398
  324.1 4.7 all-to-all-start.5
  328.9 5.8 %update_left.2 = (s16[400,2048]{1,0:T(8,128)(2,1)}, f32[2,2048]{1,0:T(2,128)}) custom-call(f32[16384,128]{1,0:T(8,128)} %get-tuple-element.78.g_ref, f32[400,4096]{1,0:T(8,128)} %bitcast.18, f32[1,4096]{1,0:T(1,128)} %bitcast.32), custom_call_target="tpu_custom_call" | custom-call | bytes 8192000 | tf_op jit(solution)/shard_map/update_left/pallas_call | solution.py:497
  334.7 12.1 %collective-permute-start.3 = (s16[400,2048]{1,0:T(8,128)(2,1)}, s16[400,2048]{1,0:T(8,128)(2,1)}, u32[]{:S(2)}, u32[]{:S(2)}) collective-permute-start(s16[400,2048]{1,0:T(8,128)(2,1)} %get-tuple-element.91), channel_id=1, source_target_pairs={{4,20},{20,4},{5,21},{21,5},{6,22},{22,6},{7,23},{23,7}} | collective-permute-start | bytes 4915208 | tf_op jit(solution)/shard_map/ppermute | solution.py:623
  346.8 1.3 collective-permute-start.2
  348.1 5.8 %update_left.3 = (s16[400,2048]{1,0:T(8,128)(2,1)}, f32[2,2048]{1,0:T(2,128)}) custom-call(f32[16384,128]{1,0:T(8,128)} %get-tuple-element.78.g_ref, f32[400,4096]{1,0:T(8,128)} %bitcast.19, f32[1,4096]{1,0:T(1,128)} %bitcast.33), custom_call_target="tpu_custom_call" | custom-call | bytes 8192000 | tf_op jit(solution)/shard_map/update_left/pallas_call | solution.py:497
  353.9 33.6 %target_grads.1.g4_ref = f32[16384,128]{1,0:T(8,128)} custom-call(s32[9,1024]{1,0:T(8,128)} %pad.21.tgt_idx, s32[9]{0:T(128)} %bitcast.40, f32[46080,128]{1,0:T(8,128)} %get-tuple-element.87.gt_ref), custom_call_target="tpu_custom_call" | custom-call | bytes 100000000 | tf_op jit(solution)/shard_map/target_grads/pallas_call | solution.py:257
  387.8 2.9 collective-permute-done.2.refs_0_
  390.8 1.1 copy-done.4
  391.9 4.4 all-to-all-start.6
  399.1 1.7 constant_dynamic-slice_fusion.t_ref
  401.7 7.2 %collective-permute-start.4 = (s16[400,2048]{1,0:T(8,128)(2,1)}, s16[400,2048]{1,0:T(8,128)(2,1)}, u32[]{:S(2)}, u32[]{:S(2)}) collective-permute-start(s16[400,2048]{1,0:T(8,128)(2,1)} %collective-permute-done.3), channel_id=1, source_target_pairs={{20,24},{4,8},{21,25},{5,9},{22,26},{6,10},{23,27},{7,11}} | collective-permute-start | bytes 4915208 | tf_op jit(solution)/shard_map/ppermute | solution.py:628
  408.8 14.5 %spread.2.g_ref = f32[400,4096]{1,0:T(8,128)} custom-call(s32[4,1,768]{2,1,0:T(1,128)} %reshape.33.idx_ref, bf16[4,400,768]{2,1,0:T(8,128)(2,1)} %copy-done.1), custom_call_target="tpu_custom_call" | custom-call | flops 10066329600 | bytes 13107200 | tf_op jit(solution)/shard_map/spread/pallas_call | solution.py:548
  423.4 16.1 %spread.3.g_ref = f32[400,4096]{1,0:T(8,128)} custom-call(f32[400,4096]{1,0:T(8,128)} %spread.2.g_ref, f32[16384,128]{1,0:T(8,128)} %target_grads.1.g4_ref, s32[4,1,768]{2,1,0:T(1,128)} %reshape.34.idx_ref, bf16[4,400,768]{2,1,0:T(8,128)(2,1)} %all-to-all-done.5.b_ref), custom_call_target="tpu_custom_call" | custom-call | flops 10066329600 | bytes 13107200 | tf_op jit(solution)/shard_map/spread/pallas_call | solution.py:548
  439.5 18.3 %all-to-all-done.6.b_ref = bf16[4,400,768]{2,1,0:T(8,128)(2,1)S(1)} async-done(((bf16[4,400,768]{2,1,0:T(8,128)(2,1)}), bf16[4,400,768]{2,1,0:T(8,128)(2,1)S(1)}, u32[]{:S(2)}, u32[]{:S(2)}) %all-to-all-start.6) | async-done | bytes 2457632 | tf_op jit(solution)/shard_map/all_to_all | solution.py:644
  457.9 1.4 copy-done.2
  459.3 10.4 %spread_update.2 = (s16[400,2048]{1,0:T(8,128)(2,1)}, f32[2,2048]{1,0:T(2,128)}) custom-call(f32[400,4096]{1,0:T(8,128)} %spread.3.g_ref, s32[4,1,768]{2,1,0:T(1,128)} %reshape.35.idx_ref, bf16[4,400,768]{2,1,0:T(8,128)(2,1)} %copy-done.2, f32[400,4096]{1,0:T(8,128)} %bitcast.26, f32[1,4096]{1,0:T(1,128)} %bitcast.45), custom_call_target="tpu_custom_call" | custom-call | flops 5033164800 | bytes 6553600 | tf_op jit(solution)/shard_map/spread_update/pallas_call | solution.py:568
  469.7 10.4 %spread_update.3 = (s16[400,2048]{1,0:T(8,128)(2,1)}, f32[2,2048]{1,0:T(2,128)}) custom-call(f32[400,4096]{1,0:T(8,128)} %spread.3.g_ref, s32[4,1,768]{2,1,0:T(1,128)} %reshape.35.idx_ref, bf16[4,400,768]{2,1,0:T(8,128)(2,1)} %copy-done.2, f32[400,4096]{1,0:T(8,128)} %bitcast.27, f32[1,4096]{1,0:T(1,128)} %bitcast.46), custom_call_target="tpu_custom_call" | custom-call | flops 5033164800 | bytes 6553600 | tf_op jit(solution)/shard_map/spread_update/pallas_call | solution.py:568
  480.1 2.1 update_relations.1
  482.2 4.3 collective-permute-start.8
  486.5 1.3 collective-permute-start.7
  487.9 41.7 %collective-permute-done.8 = s16[400,2048]{1,0:T(8,128)(2,1)} collective-permute-done((s16[400,2048]{1,0:T(8,128)(2,1)}, s16[400,2048]{1,0:T(8,128)(2,1)}, u32[]{:S(2)}, u32[]{:S(2)}) %collective-permute-start.8) | collective-permute-done | bytes 1638432 | tf_op jit(solution)/shard_map/ppermute | solution.py:623
  529.5 2.5 collective-permute-start.9
  532.8 2.1 all-gather.2.cloned.1.call-done.g_ref
  534.8 4.0 join_relations.1
  539.4 4.4 decode.4.refs_1_
  543.8 4.0 decode.5
  547.8 4.1 collective-permute-done.6.refs_0_
  553.2 4.4 decode.6.refs_1_
  557.6 4.0 decode.7
  (79 shorter events, 12.2 us)
Async XLA Ops:
  18.0 0.6 copy-start.7
  35.7 60.7 %all-to-all-start.1 = ((bf16[4,400,768]{2,1,0:T(8,128)(2,1)}), bf16[4,400,768]{2,1,0:T(8,128)(2,1)S(1)}, u32[]{:S(2)}, u32[]{:S(2)}) async-start(bf16[4,400,768]{2,1,0:T(8,128)(2,1)} %serve.3), calls=%async_computation.1 | async-start | bytes 4915200 | tf_op jit(solution)/shard_map/all_to_all | solution.py:644
  96.4 5.9 %copy-start.11 = (s32[9,1000]{1,0:T(8,128)S(1)}, s32[9,1000]{1,0:T(8,128)}, u32[]{:S(2)}) copy-start(s32[9,1000]{1,0:T(8,128)} %param.17) | copy-start | bytes 108004
  96.4 6.6 %copy-start.12 = (s32[9,1000]{1,0:T(8,128)S(1)}, s32[9,1000]{1,0:T(8,128)}, u32[]{:S(2)}) copy-start(s32[9,1000]{1,0:T(8,128)} %param.18) | copy-start | bytes 108004
  96.4 7.2 %copy-start.13 = (s32[9,1000]{1,0:T(8,128)S(1)}, s32[9,1000]{1,0:T(8,128)}, u32[]{:S(2)}) copy-start(s32[9,1000]{1,0:T(8,128)} %param.19) | copy-start | bytes 108004
  96.4 1.4 copy-start.3
  97.8 84.9 %all-to-all-start.3 = ((bf16[4,400,768]{2,1,0:T(8,128)(2,1)}), bf16[4,400,768]{2,1,0:T(8,128)(2,1)S(1)}, u32[]{:S(2)}, u32[]{:S(2)}) async-start(bf16[4,400,768]{2,1,0:T(8,128)(2,1)} %serve.4), calls=%async_computation.3 | async-start | bytes 4915200 | tf_op jit(solution)/shard_map/all_to_all | solution.py:644
  182.8 21.9 %copy-start = (bf16[4,400,768]{2,1,0:T(8,128)(2,1)}, bf16[4,400,768]{2,1,0:T(8,128)(2,1)S(1)}, u32[]{:S(2)}) copy-start(bf16[4,400,768]{2,1,0:T(8,128)(2,1)S(1)} %all-to-all-done.3.neg_ref) | copy-start | bytes 7372804
  182.8 64.9 %all-to-all-start.2 = ((bf16[4,400,768]{2,1,0:T(8,128)(2,1)}), bf16[4,400,768]{2,1,0:T(8,128)(2,1)}, u32[]{:S(2)}, u32[]{:S(2)}) async-start(bf16[4,400,768]{2,1,0:T(8,128)(2,1)} %serve.5), calls=%async_computation.2 | async-start | bytes 4915200 | tf_op jit(solution)/shard_map/all_to_all | solution.py:644
  247.7 76.4 %all-to-all-start.4 = ((bf16[4,400,768]{2,1,0:T(8,128)(2,1)}), bf16[4,400,768]{2,1,0:T(8,128)(2,1)S(1)}, u32[]{:S(2)}, u32[]{:S(2)}) async-start(bf16[4,400,768]{2,1,0:T(8,128)(2,1)} %get-tuple-element.85), calls=%async_computation.4 | async-start | bytes 4915200 | tf_op jit(solution)/shard_map/all_to_all | solution.py:644
  324.1 10.6 %copy-start.1 = (bf16[4,400,768]{2,1,0:T(8,128)(2,1)}, bf16[4,400,768]{2,1,0:T(8,128)(2,1)S(1)}, u32[]{:S(2)}) copy-start(bf16[4,400,768]{2,1,0:T(8,128)(2,1)S(1)} %all-to-all-done.4.b_ref) | copy-start | bytes 7372804
  324.1 66.6 %all-to-all-start.5 = ((bf16[4,400,768]{2,1,0:T(8,128)(2,1)}), bf16[4,400,768]{2,1,0:T(8,128)(2,1)}, u32[]{:S(2)}, u32[]{:S(2)}) async-start(bf16[4,400,768]{2,1,0:T(8,128)(2,1)} %get-tuple-element.90), calls=%async_computation.5 | async-start | bytes 4915200 | tf_op jit(solution)/shard_map/all_to_all | solution.py:644
  328.9 94.4 %reduce-scatter.2.cloned.1.call-start = ((), (), s32[]{:S(2)}) async-start(), calls=%async_computation.8 | async-start | bytes 3244032 | tf_op jit(solution)/shard_map/reduce_scatter | solution.py:713
  334.7 53.1 %collective-permute-start.3 = (s16[400,2048]{1,0:T(8,128)(2,1)}, s16[400,2048]{1,0:T(8,128)(2,1)}, u32[]{:S(2)}, u32[]{:S(2)}) collective-permute-start(s16[400,2048]{1,0:T(8,128)(2,1)} %get-tuple-element.91), channel_id=1, source_target_pairs={{4,20},{20,4},{5,21},{21,5},{6,22},{22,6},{7,23},{23,7}} | collective-permute-start | bytes 4915208 | tf_op jit(solution)/shard_map/ppermute | solution.py:623
  346.8 44.0 %collective-permute-start.2 = (s16[400,2048]{1,0:T(8,128)(2,1)}, s16[400,2048]{1,0:T(8,128)(2,1)S(1)}, u32[]{:S(2)}, u32[]{:S(2)}) collective-permute-start(s16[400,2048]{1,0:T(8,128)(2,1)} %get-tuple-element.91), channel_id=1, source_target_pairs={{0,20},{8,28},{12,0},{16,4},{24,12},{28,16},{1,21},{9,29},{13,1},{... | collective-permute-start | bytes 4915208 | tf_op jit(solution)/shard_map/ppermute | solution.py:624
  387.4 8.9 %copy-start.17 = (f32[1345]{0:T(1024)S(1)}, f32[1345]{0:T(1024)}, u32[]{:S(2)}) copy-start(f32[1345]{0:T(1024)} %param.16) | copy-start | bytes 16144
  387.4 9.8 %copy-start.8 = (s32[4,9,256]{2,1,0:T(8,128)S(1)}, s32[4,9,256]{2,1,0:T(8,128)}, u32[]{:S(2)}) copy-start(s32[4,9,256]{2,1,0:T(8,128)} %copy-done.7) | copy-start | bytes 110596
  390.8 1.2 copy-start.4
  390.8 10.1 %copy-start.14 = (f32[2,2048]{1,0:T(2,128)S(1)}, f32[2,2048]{1,0:T(2,128)}, u32[]{:S(2)}) copy-start(f32[2,2048]{1,0:T(2,128)} %get-tuple-element.81) | copy-start | bytes 49156
  390.8 10.1 %copy-start.15 = (f32[2,2048]{1,0:T(2,128)S(1)}, f32[2,2048]{1,0:T(2,128)}, u32[]{:S(2)}) copy-start(f32[2,2048]{1,0:T(2,128)} %get-tuple-element.82) | copy-start | bytes 49156
  391.9 65.9 %all-to-all-start.6 = ((bf16[4,400,768]{2,1,0:T(8,128)(2,1)}), bf16[4,400,768]{2,1,0:T(8,128)(2,1)S(1)}, u32[]{:S(2)}, u32[]{:S(2)}) async-start(bf16[4,400,768]{2,1,0:T(8,128)(2,1)} %get-tuple-element.95), calls=%async_computation.6 | async-start | bytes 4915200 | tf_op jit(solution)/shard_map/all_to_all | solution.py:644
  396.3 83.7 %all-reduce.7.cloned.1.call-start = ((), (), s32[]{:S(2)}) async-start(), calls=%async_computation.9 | async-start | bytes 720896 | tf_op jit(solution)/shard_map/psum | solution.py:726
  400.8 38.7 %collective-permute-start = (f32[2,4096]{1,0:T(2,128)S(1)}, f32[2,4096]{1,0:T(2,128)S(1)}, u32[]{:S(2)}, u32[]{:S(2)}) collective-permute-start(f32[2,4096]{1,0:T(2,128)S(1)} %pad_maximum_fusion), channel_id=1, source_target_pairs={{12,0},{16,4},{20,8},{24,12},{28,16},{0,20},{4,24},{8,28},{13,1},{... | collective-permute-start | bytes 98312 | tf_op jit(solution)/shard_map/ppermute | solution.py:612
  401.6 37.9 %collective-permute-start.1 = (s16[400,2048]{1,0:T(8,128)(2,1)}, s16[400,2048]{1,0:T(8,128)(2,1)}, u32[]{:S(2)}, u32[]{:S(2)}) collective-permute-start(s16[400,2048]{1,0:T(8,128)(2,1)} %get-tuple-element.83), channel_id=1, source_target_pairs={{12,0},{16,4},{20,8},{24,12},{28,16},{0,20},{4,24},{8,28},{13,1},{... | collective-permute-start | bytes 4915208 | tf_op jit(solution)/shard_map/ppermute | solution.py:612
  401.7 37.9 %collective-permute-start.4 = (s16[400,2048]{1,0:T(8,128)(2,1)}, s16[400,2048]{1,0:T(8,128)(2,1)}, u32[]{:S(2)}, u32[]{:S(2)}) collective-permute-start(s16[400,2048]{1,0:T(8,128)(2,1)} %collective-permute-done.3), channel_id=1, source_target_pairs={{20,24},{4,8},{21,25},{5,9},{22,26},{6,10},{23,27},{7,11}} | collective-permute-start | bytes 4915208 | tf_op jit(solution)/shard_map/ppermute | solution.py:628
  423.3 111.5 %all-gather.2.cloned.1.call-start = ((), (), s32[]{:S(2)}) async-start(), calls=%async_computation.10 | async-start | bytes 3244032 | tf_op jit(solution)/shard_map/all_gather | solution.py:745
  439.5 99.3 %copy-start.9 = (f32[2,4096]{1,0:T(2,128)}, f32[2,4096]{1,0:T(2,128)S(1)}, u32[]{:S(2)}) copy-start(f32[2,4096]{1,0:T(2,128)S(1)} %collective-permute-done.m_ref) | copy-start | bytes 98308
  457.9 1.4 copy-start.2
  469.7 62.3 %copy-start.16 = (f32[2,2048]{1,0:T(2,128)S(1)}, f32[2,2048]{1,0:T(2,128)}, u32[]{:S(2)}) copy-start(f32[2,2048]{1,0:T(2,128)} %get-tuple-element.96) | copy-start | bytes 49156
  482.2 47.3 %collective-permute-start.8 = (s16[400,2048]{1,0:T(8,128)(2,1)}, s16[400,2048]{1,0:T(8,128)(2,1)}, u32[]{:S(2)}, u32[]{:S(2)}) collective-permute-start(s16[400,2048]{1,0:T(8,128)(2,1)} %get-tuple-element.106), channel_id=1, source_target_pairs={{4,20},{20,4},{5,21},{21,5},{6,22},{22,6},{7,23},{23,7}} | collective-permute-start | bytes 4915208 | tf_op jit(solution)/shard_map/ppermute | solution.py:623
  486.5 61.3 %collective-permute-start.7 = (s16[400,2048]{1,0:T(8,128)(2,1)}, s16[400,2048]{1,0:T(8,128)(2,1)S(1)}, u32[]{:S(2)}, u32[]{:S(2)}) collective-permute-start(s16[400,2048]{1,0:T(8,128)(2,1)} %get-tuple-element.106), channel_id=1, source_target_pairs={{0,20},{8,28},{12,0},{16,4},{24,12},{28,16},{1,21},{9,29},{13,1},{... | collective-permute-start | bytes 4915208 | tf_op jit(solution)/shard_map/ppermute | solution.py:624
  487.8 64.1 %collective-permute-start.6 = (s16[400,2048]{1,0:T(8,128)(2,1)}, s16[400,2048]{1,0:T(8,128)(2,1)S(1)}, u32[]{:S(2)}, u32[]{:S(2)}) collective-permute-start(s16[400,2048]{1,0:T(8,128)(2,1)} %get-tuple-element.104), channel_id=1, source_target_pairs={{12,0},{16,4},{20,8},{24,12},{28,16},{0,20},{4,24},{8,28},{13,1},{... | collective-permute-start | bytes 4915208 | tf_op jit(solution)/shard_map/ppermute | solution.py:612
  529.5 23.7 %collective-permute-start.9 = (s16[400,2048]{1,0:T(8,128)(2,1)}, s16[400,2048]{1,0:T(8,128)(2,1)}, u32[]{:S(2)}, u32[]{:S(2)}) collective-permute-start(s16[400,2048]{1,0:T(8,128)(2,1)} %collective-permute-done.8), channel_id=1, source_target_pairs={{20,24},{4,8},{21,25},{5,9},{22,26},{6,10},{23,27},{7,11}} | collective-permute-start | bytes 4915208 | tf_op jit(solution)/shard_map/ppermute | solution.py:628
  538.8 13.8 %collective-permute-start.5 = (f32[2,4096]{1,0:T(2,128)S(1)}, f32[2,4096]{1,0:T(2,128)S(1)}, u32[]{:S(2)}, u32[]{:S(2)}) collective-permute-start(f32[2,4096]{1,0:T(2,128)S(1)} %pad_maximum_fusion.1), channel_id=1, source_target_pairs={{12,0},{16,4},{20,8},{24,12},{28,16},{0,20},{4,24},{8,28},{13,1},{... | collective-permute-start | bytes 98312 | tf_op jit(solution)/shard_map/ppermute | solution.py:612
  543.8 8.1 %copy-start.18 = (f32[1,1345]{1,0:T(1,128)S(1)}, f32[1,1345]{1,0:T(1,128)}, u32[]{:S(2)}) copy-start(f32[1,1345]{1,0:T(1,128)} %get-tuple-element.109) | copy-start | bytes 16144
  547.8 5.4 copy-start.5
  551.9 5.7 %copy-start.6 = (s16[400,2048]{1,0:T(8,128)(2,1)}, s16[400,2048]{1,0:T(8,128)(2,1)S(1)}, u32[]{:S(2)}) copy-start(s16[400,2048]{1,0:T(8,128)(2,1)S(1)} %collective-permute-done.6.refs_0_) | copy-start | bytes 4915204
  552.6 0.6 copy-start.10
Sparse Core Ops, SparseCore 0:
  348.2 52.5 reduce-scatter.1
  423.4 52.8 all-reduce.6
  482.3 52.4 all-gather.1
